TPU v7x, 32 devices: a whole 2x2x4 slice. The times are simulated.
32 devices in a mesh: section: 2 (over x), fsdp: 16 (over z, y, core).
Axes of the slice: x: 2, y: 2, z: 4, core: 2. Of those that a mesh axis runs over, the one named last changes fastest.
Arguments:
- section_inputs: bfloat16 [2, 4, 32, 128, 768], P('section', None, 'fsdp'), may hold values from -6 to 6
- norm_gains: bfloat16 [2, 2, 768], P('section', None, 'fsdp'), may hold values from 0.5 to 1.5
- offsets: bfloat16 [2, 6, 768], P('section', None, 'fsdp'), may hold values from -2 to 2
- attend_weight: bfloat16 [2, 768, 2304], P('section', 'fsdp'), may hold values from -0.21875 to 0.21875
- merge_weight: bfloat16 [2, 768, 768], P('section', 'fsdp'), may hold values from -0.875 to 0.875
- up_weight: bfloat16 [2, 768, 3072], P('section', 'fsdp'), may hold values from -0.21875 to 0.21875
- up_bias: bfloat16 [2, 3072], P('section', 'fsdp'), may hold values from -2 to 2
- down_weight: bfloat16 [2, 3072, 768], P('section', 'fsdp'), may hold values from -0.109375 to 0.109375
Outputs:
- section_outputs: bfloat16 [2, 4, 32, 128, 768], P('section', None, 'fsdp')
- gains_grad: float32 [2, 2, 768], P('section', None, 'fsdp')
- offsets_grad: float32 [2, 6, 768], P('section', None, 'fsdp')
- attend_grad: float32 [2, 768, 2304], P('section', 'fsdp')
- merge_grad: float32 [2, 768, 768], P('section', 'fsdp')
- up_grad: float32 [2, 768, 3072], P('section', 'fsdp')
- bias_grad: float32 [2, 3072], P('section', 'fsdp')
- down_grad: float32 [2, 3072, 768], P('section', 'fsdp')
All inputs are finite; a program needn't handle non-finite values.
Results may differ from a plain program's by a relative error of at most 0.009.
Values may be sent and summed in bfloat16 or wider, within the bound.
A program may use at most 256 MiB of HBM per device.

v0:
```python
import jax
import jax.numpy as jnp
from jax import lax
from jax.sharding import PartitionSpec as P

HEADS = 12
HEAD_DIM = 64


epsilon = 1e-05


def from_behind(block, axis, distance):
    devices = range(lax.axis_size(axis))
    route = [(i - distance, i) for i in devices if i - distance in devices]
    return lax.ppermute(block, axis, route)


def normalize(features, gain_row, offset):
    centred = features - jnp.mean(features, axis=-1, keepdims=True)
    spread = jnp.mean(centred * centred, axis=-1, keepdims=True)
    return centred * lax.rsqrt(spread + epsilon) * gain_row + offset


def gelu_exact(features):
    return jax.nn.gelu(features, approximate=False)


def split_heads(matrix, clip_count):
    return matrix.reshape(clip_count, matrix.shape[0] // clip_count, HEADS, HEAD_DIM)


def layer_forward(hidden, weights, clip_count):
    attend_weight, merge_weight, up_weight, down_weight, gain_rows, offset_rows, up_bias = weights
    gain_rows = gain_rows.astype(jnp.float32)
    offset_rows = offset_rows.astype(jnp.float32)
    row_count, model_width = hidden.shape
    score_scale = HEAD_DIM ** (-0.5)
    normed = normalize(hidden, gain_rows[0], offset_rows[0]).astype(jnp.bfloat16)
    projected = jnp.dot(normed, attend_weight, preferred_element_type=jnp.float32)
    query_heads = split_heads(
        (projected[:, :model_width] + offset_rows[2]).astype(jnp.bfloat16), clip_count
    )
    key_heads = split_heads(
        projected[:, model_width : 2 * model_width].astype(jnp.bfloat16), clip_count
    )
    value_heads = split_heads(
        (projected[:, 2 * model_width :] + offset_rows[3]).astype(jnp.bfloat16), clip_count
    )
    scores = (
        jnp.einsum("clhe,cmhe->chlm", query_heads, key_heads, preferred_element_type=jnp.float32)
        * score_scale
    )
    row_peak = jnp.max(scores, axis=-1, keepdims=True)
    exponent = jnp.exp(scores - row_peak)
    row_total = jnp.sum(exponent, axis=-1, keepdims=True)
    probability = (exponent / row_total).astype(jnp.bfloat16)
    log_total = (row_peak + jnp.log(row_total))[..., 0]
    attended = jnp.einsum(
        "chlm,cmhe->clhe", probability, value_heads, preferred_element_type=jnp.float32
    )
    attended = attended.reshape(row_count, model_width).astype(jnp.bfloat16)
    middle = (
        hidden
        + jnp.dot(attended, merge_weight, preferred_element_type=jnp.float32)
        + offset_rows[4]
    )
    normed_two = normalize(middle, gain_rows[1], offset_rows[1]).astype(jnp.bfloat16)
    raised = jnp.dot(normed_two, up_weight, preferred_element_type=jnp.float32) + up_bias.astype(
        jnp.float32
    )
    activated = gelu_exact(raised).astype(jnp.bfloat16)
    result = (
        middle
        + jnp.dot(activated, down_weight, preferred_element_type=jnp.float32)
        + offset_rows[5]
    )
    saved_state = (
        hidden,
        normed,
        query_heads,
        key_heads,
        value_heads,
        log_total,
        attended,
        middle,
        normed_two,
        raised,
        activated,
    )
    return (result, saved_state)


def layer_backward(out_grad, saved_state, weights, clip_count):
    attend_weight, merge_weight, up_weight, down_weight, gain_rows, offset_rows, up_bias = weights
    gain_rows = gain_rows.astype(jnp.float32)
    offset_rows = offset_rows.astype(jnp.float32)
    (
        hidden,
        normed,
        query_heads,
        key_heads,
        value_heads,
        log_total,
        attended,
        middle,
        normed_two,
        raised,
        activated,
    ) = saved_state
    row_count, model_width = hidden.shape
    score_scale = HEAD_DIM ** (-0.5)
    low_grad = out_grad.astype(jnp.bfloat16)
    down_term = jnp.einsum("tf,td->fd", activated, low_grad, preferred_element_type=jnp.float32)
    last_bias = jnp.sum(out_grad, axis=0)
    act_grad = jnp.einsum("td,fd->tf", low_grad, down_weight, preferred_element_type=jnp.float32)
    raised_grad = jax.vjp(gelu_exact, raised)[1](act_grad)[0]
    up_bias_term = jnp.sum(raised_grad, axis=0)
    raised_low = raised_grad.astype(jnp.bfloat16)
    up_term = jnp.einsum("td,tf->df", normed_two, raised_low, preferred_element_type=jnp.float32)
    normed_two_grad = jnp.einsum(
        "tf,df->td", raised_low, up_weight, preferred_element_type=jnp.float32
    )
    second_back = jax.vjp(normalize, middle, gain_rows[1], offset_rows[1])[1]
    middle_part, gain_two, offset_two = second_back(normed_two_grad)
    middle_grad = out_grad + middle_part
    merge_bias = jnp.sum(middle_grad, axis=0)
    middle_low = middle_grad.astype(jnp.bfloat16)
    merge_term = jnp.einsum("td,te->de", attended, middle_low, preferred_element_type=jnp.float32)
    attended_grad = jnp.einsum(
        "te,de->td", middle_low, merge_weight, preferred_element_type=jnp.float32
    )
    attended_grad = split_heads(attended_grad.astype(jnp.bfloat16), clip_count)
    scores = (
        jnp.einsum("clhe,cmhe->chlm", query_heads, key_heads, preferred_element_type=jnp.float32)
        * score_scale
    )
    probability = jnp.exp(scores - log_total[..., None])
    prob_grad = jnp.einsum(
        "clhe,cmhe->chlm", attended_grad, value_heads, preferred_element_type=jnp.float32
    )
    value_grad = jnp.einsum(
        "chlm,clhe->cmhe",
        probability.astype(jnp.bfloat16),
        attended_grad,
        preferred_element_type=jnp.float32,
    )
    score_grad = probability * (
        prob_grad - jnp.sum(prob_grad * probability, axis=-1, keepdims=True)
    )
    score_grad = score_grad.astype(jnp.bfloat16)
    query_grad = (
        jnp.einsum("chlm,cmhe->clhe", score_grad, key_heads, preferred_element_type=jnp.float32)
        * score_scale
    )
    key_grad = (
        jnp.einsum("chlm,clhe->cmhe", score_grad, query_heads, preferred_element_type=jnp.float32)
        * score_scale
    )
    query_grad = query_grad.reshape(row_count, model_width)
    key_grad = key_grad.reshape(row_count, model_width)
    value_grad = value_grad.reshape(row_count, model_width)
    query_bias = jnp.sum(query_grad, axis=0)
    value_bias = jnp.sum(value_grad, axis=0)
    joined_low = jnp.concatenate([query_grad, key_grad, value_grad], axis=1).astype(jnp.bfloat16)
    attend_term = jnp.einsum("td,te->de", normed, joined_low, preferred_element_type=jnp.float32)
    normed_grad = jnp.einsum(
        "te,de->td", joined_low, attend_weight, preferred_element_type=jnp.float32
    )
    first_back = jax.vjp(normalize, hidden, gain_rows[0], offset_rows[0])[1]
    hidden_part, gain_one, offset_one = first_back(normed_grad)
    hidden_grad = middle_grad + hidden_part
    gain_term = jnp.stack([gain_one, gain_two])
    offset_term = jnp.stack([offset_one, offset_two, query_bias, value_bias, merge_bias, last_bias])
    return (
        hidden_grad,
        (attend_term, merge_term, up_term, down_term, gain_term, offset_term, up_bias_term),
    )


def body(
    section_inputs,
    norm_gains,
    offsets,
    attend_weight,
    merge_weight,
    up_weight,
    up_bias,
    down_weight,
):
    shards = (attend_weight, merge_weight, up_weight, down_weight, norm_gains, offsets, up_bias)
    gathered = (
        lax.all_gather(shards[0], "fsdp", axis=1, tiled=True),
        lax.all_gather(shards[1], "fsdp", axis=1, tiled=True),
        lax.all_gather(shards[2], "fsdp", axis=1, tiled=True),
        lax.all_gather(shards[3], "fsdp", axis=1, tiled=True),
        lax.all_gather(shards[4], "fsdp", axis=2, tiled=True),
        lax.all_gather(shards[5], "fsdp", axis=2, tiled=True),
        lax.all_gather(shards[6], "fsdp", axis=1, tiled=True),
    )
    weights = tuple((tensor[0] for tensor in gathered))
    is_first = lax.axis_index("section") == 0
    own_data = section_inputs[0]
    batches, clip_count, length, model_width = own_data.shape
    row_count = clip_count * length
    own_rows = own_data.reshape(batches, row_count, model_width)
    kept_state = []
    upper_rows = []
    received = jnp.zeros((row_count, model_width), jnp.bfloat16)
    for instant in range(batches + 1):
        entering = jnp.where(is_first, own_rows[min(instant, batches - 1)], received)
        result, saved_state = layer_forward(entering.astype(jnp.float32), weights, clip_count)
        kept_state.append(saved_state)
        rounded = result.astype(jnp.bfloat16)
        if instant >= 1:
            upper_rows.append(rounded)
        if instant < batches:
            received = from_behind(rounded, "section", 1)
    gathered = (
        lax.all_gather(shards[0], "fsdp", axis=1, tiled=True),
        lax.all_gather(shards[1], "fsdp", axis=1, tiled=True),
        lax.all_gather(shards[2], "fsdp", axis=1, tiled=True),
        lax.all_gather(shards[3], "fsdp", axis=1, tiled=True),
        lax.all_gather(shards[4], "fsdp", axis=2, tiled=True),
        lax.all_gather(shards[5], "fsdp", axis=2, tiled=True),
        lax.all_gather(shards[6], "fsdp", axis=1, tiled=True),
    )
    weights = tuple((tensor[0] for tensor in gathered))
    totals = (
        jnp.zeros(weights[0].shape, jnp.float32),
        jnp.zeros(weights[1].shape, jnp.float32),
        jnp.zeros(weights[2].shape, jnp.float32),
        jnp.zeros(weights[3].shape, jnp.float32),
        jnp.zeros(weights[4].shape, jnp.float32),
        jnp.zeros(weights[5].shape, jnp.float32),
        jnp.zeros(weights[6].shape, jnp.float32),
    )
    received_grad = jnp.zeros((row_count, model_width), jnp.bfloat16)
    lower_rows = []
    for instant in range(batches + 1):
        position = batches - 1 - instant
        if position >= 0:
            own_grad = own_rows[position]
        else:
            own_grad = jnp.zeros((row_count, model_width), jnp.bfloat16)
        cotangent = jnp.where(is_first, received_grad, own_grad).astype(jnp.float32)
        hidden_grad, param_terms = layer_backward(
            cotangent, kept_state[batches - instant], weights, clip_count
        )
        totals = jax.tree.map(jnp.add, totals, param_terms)
        rounded = hidden_grad.astype(jnp.bfloat16)
        if instant >= 1:
            lower_rows.append(rounded)
        if instant < batches:
            received_grad = from_behind(rounded, "section", -1)
    ordered_lower = lower_rows[::-1]
    combined = jnp.stack(
        [
            jnp.where(is_first, lower_part, upper_part)
            for lower_part, upper_part in zip(ordered_lower, upper_rows)
        ]
    )
    section_outputs = combined.reshape(1, batches, clip_count, length, model_width)
    reduced = (
        lax.psum_scatter(totals[0][None], "fsdp", scatter_dimension=1, tiled=True),
        lax.psum_scatter(totals[1][None], "fsdp", scatter_dimension=1, tiled=True),
        lax.psum_scatter(totals[2][None], "fsdp", scatter_dimension=1, tiled=True),
        lax.psum_scatter(totals[3][None], "fsdp", scatter_dimension=1, tiled=True),
        lax.psum_scatter(totals[4][None], "fsdp", scatter_dimension=2, tiled=True),
        lax.psum_scatter(totals[5][None], "fsdp", scatter_dimension=2, tiled=True),
        lax.psum_scatter(totals[6][None], "fsdp", scatter_dimension=1, tiled=True),
    )
    return (
        section_outputs,
        reduced[4],
        reduced[5],
        reduced[0],
        reduced[1],
        reduced[2],
        reduced[6],
        reduced[3],
    )


def solution(mesh):
    return jax.shard_map(
        body,
        mesh=mesh,
        in_specs=(
            P("section", None, "fsdp", None, None),
            P("section", None, "fsdp"),
            P("section", None, "fsdp"),
            P("section", "fsdp", None),
            P("section", "fsdp", None),
            P("section", "fsdp", None),
            P("section", "fsdp"),
            P("section", "fsdp", None),
        ),
        out_specs=(
            P("section", None, "fsdp", None, None),
            P("section", None, "fsdp"),
            P("section", None, "fsdp"),
            P("section", "fsdp", None),
            P("section", "fsdp", None),
            P("section", "fsdp", None),
            P("section", "fsdp"),
            P("section", "fsdp", None),
        ),
        check_vma=False,
    )
```

profile of v0, /device:TPU:0, one launch (start us, length us, event | category | flops | bytes accessed | tf_op | source)
XLA Modules:
  0.0 1128.7 jit_solution(18355625509491006847)
XLA Ops:
  12.9 35.9 %all-reduce = bf16[3072]{0:T(1024)(128)(2,1)S(1)} all-reduce(bf16[3072]{0:T(1024)(128)(2,1)S(1)} %dynamic-update-slice), channel_id=1, replica_groups=mesh['section'=2,'fsdp'=16] {'fsdp'}, use_global_device_ids=true, to_apply=%add | all-reduce | flops 3072 | bytes 12288
  50.9 19.2 %all_gather.27 = bf16[1,6,768]{1,0,2:T(2,128)(2,1)S(1)} all-gather(bf16[1,6,48]{1,0,2:T(2,128)(2,1)S(1)} %copy.279), channel_id=1, replica_groups=mesh['section'=2,'fsdp'=16] {'fsdp'}, dimensions={2}, use_global_device_ids=true | all-gather | bytes 9792 | tf_op jit(solution)/shard_map/all_gather | solution.py:198
  70.5 19.9 %all_gather.26 = bf16[1,2,768]{1,0,2:T(2,128)(2,1)S(1)} all-gather(bf16[1,2,48]{1,0,2:T(2,128)(2,1)S(1)} %copy.278), channel_id=1, replica_groups=mesh['section'=2,'fsdp'=16] {'fsdp'}, dimensions={2}, use_global_device_ids=true | all-gather | bytes 3264 | tf_op jit(solution)/shard_map/all_gather | solution.py:197
  100.2 13.6 %slice_reduce_fusion = (f32[768]{0:T(1024)}, f32[768]{0:T(1024)S(1)}, f32[768]{0:T(1024)}, f32[768]{0:T(1024)}, f32[768]{0:T(1024)}, /*index=5*/f32[768]{0:T(1024)S(1)}) fusion(f32[1,6,768]{1,0,2:T(1,128)S(1)} %convert_element_type.339), kind=kLoop, calls=%fused_computation.466 | loop fusion | bytes 36864 | tf_op jit(solution)/shard_map/slice | solution.py:76
  122.5 34.0 %all-gather.9.cloned.1.call-done = bf16[1,768,3072]{2,1,0:T(8,128)(2,1)} async-done(((bf16[1,48,3072]{2,1,0:T(8,128)(2,1)}), bf16[1,768,3072]{2,1,0:T(8,128)(2,1)}) %all-gather.9.cloned.1.call-update) | async-done | bytes 4718608 | tf_op jit(solution)/shard_map/all_gather | solution.py:195
  156.5 11.8 %multiply_convert_fusion.4 = (bf16[256,3072]{1,0:T(8,128)(2,1)}, f32[256,3072]{1,0:T(8,128)}, f32[256,3072]{1,0:T(8,128)}) fusion(f32[3072]{0:T(1024)S(1)} %copy-done.269, bf16[1,768,3072]{2,1,0:T(8,128)(2,1)} %all-gather.9.cloned.1.call-done, f32[256,768]{1,0:T(8,128)S(1)} %get-tuple-element.138, f32[768]{0:T(1024)S(1)} %get-tuple-element.52, ...), kind=kOutput, calls=%fused_computation.136 | convolution fusion | flops 1260847104 | bytes 13389824 | tf_op jit(solution)/shard_map/dot_general | solution.py:69
  168.2 42.3 %all-gather.11.cloned.1.call-done = bf16[1,3072,768]{2,1,0:T(8,128)(2,1)} async-done(((bf16[1,192,768]{2,1,0:T(8,128)(2,1)}), bf16[1,3072,768]{2,1,0:T(8,128)(2,1)}) %all-gather.11.cloned.1.call-update) | async-done | bytes 4718608 | tf_op jit(solution)/shard_map/all_gather | solution.py:196
  218.3 8.8 collective-permute-done
  239.6 11.4 %multiply_convert_fusion.3 = (bf16[256,3072]{1,0:T(8,128)(2,1)S(1)}, f32[256,3072]{1,0:T(8,128)}, f32[256,3072]{1,0:T(8,128)}) fusion(f32[3072]{0:T(1024)S(1)} %copy-done.270, bf16[1,768,3072]{2,1,0:T(8,128)(2,1)S(1)} %bitcast.569, f32[256,768]{1,0:T(8,128)S(1)} %get-tuple-element.143, f32[256]{0:T(256)S(1)} %fusion.394, ...), kind=kOutput, calls=%fused_computation.123 | convolution fusion | flops 1260847104 | bytes 13389824 | tf_op jit(solution)/shard_map/dot_general | solution.py:69
  257.1 7.9 collective-permute-done.1
  274.7 11.1 multiply_convert_fusion.2
  309.4 11.1 multiply_convert_fusion.1
  353.2 11.1 multiply_convert_fusion
  404.5 6.2 collective-permute-done.4
  582.4 11.0 add_bitcast_fusion.2
  594.6 6.8 fusion.298
  617.1 17.9 %add_bitcast_fusion.1 = f32[1,768,3072]{2,1,0:T(8,128)} fusion(f32[768,3072]{1,0:T(8,128)} %fusion.286, f32[768,3072]{1,0:T(8,128)} %fusion.290, f32[768,3072]{1,0:T(8,128)} %fusion.298, f32[768,3072]{1,0:T(8,128)} %fusion.294, bf16[256,3072]{1,0:T(8,128)(2,1)S(1)} %copy-done.136, f32[256,768]{1,0:T(8,128)S(1)} %copy-done.58, ...), kind=kOutput, calls=%fused_computation.1 | convolution fusion | flops 1218379776 | bytes 49553408 | tf_op jit(solution)/shard_map/td,tf->df/dot_general | solution.py:120
  636.0 6.7 fusion.468
  657.8 17.4 %add_bitcast_fusion = f32[1,3072,768]{2,1,0:T(8,128)} fusion(f32[3072,768]{1,0:T(8,128)} %fusion.471, f32[3072,768]{1,0:T(8,128)} %fusion.470, f32[3072,768]{1,0:T(8,128)} %fusion.468, f32[3072,768]{1,0:T(8,128)} %fusion.469, bf16[256,3072]{1,0:T(8,128)(2,1)S(1)} %copy-done.108, bf16[256,768]{1,0:T(8,128)(2,1)S(1)} %copy-done.34, pred[]{:T(512)S(6)} %eq.3), kind=kOutput, calls=%fused_computation | convolution fusion | flops 1217593344 | bytes 49152000 | tf_op jit(solution)/shard_map/tf,td->fd/dot_general | solution.py:114
  685.9 43.7 %reduce-scatter.24.cloned.1.call-done = f32[48,6]{1,0:T(8,128)} async-done(((f32[768,6]{1,0:T(8,128)}), f32[48,6]{1,0:T(8,128)}) %reduce-scatter.24.cloned.1.call-update) | async-done | bytes 1168
  731.1 65.3 %reduce-scatter.16.cloned.1.call-done = f32[1,48,768]{2,1,0:T(8,128)} async-done(((f32[1,768,768]{2,1,0:T(8,128)}), f32[1,48,768]{2,1,0:T(8,128)}) %reduce-scatter.16.cloned.1.call-update) | async-done | bytes 147472 | tf_op jit(solution)/shard_map/reduce_scatter | solution.py:266
  796.5 93.7 %reduce-scatter.14.cloned.1.call-done = f32[1,48,2304]{2,1,0:T(8,128)} async-done(((f32[1,768,2304]{2,1,0:T(8,128)}), f32[1,48,2304]{2,1,0:T(8,128)}) %reduce-scatter.14.cloned.1.call-update) | async-done | bytes 442384 | tf_op jit(solution)/shard_map/reduce_scatter | solution.py:265
  890.2 115.9 %reduce-scatter.18.cloned.1.call-done = f32[1,48,3072]{2,1,0:T(8,128)} async-done(((f32[1,768,3072]{2,1,0:T(8,128)}), f32[1,48,3072]{2,1,0:T(8,128)}) %reduce-scatter.18.cloned.1.call-update) | async-done | bytes 589840 | tf_op jit(solution)/shard_map/reduce_scatter | solution.py:267
  1006.1 115.8 %reduce-scatter.20.cloned.1.call-done = f32[1,192,768]{2,1,0:T(8,128)} async-done(((f32[1,3072,768]{2,1,0:T(8,128)}), f32[1,192,768]{2,1,0:T(8,128)}) %reduce-scatter.20.cloned.1.call-update) | async-done | bytes 589840 | tf_op jit(solution)/shard_map/reduce_scatter | solution.py:268
  (1098 shorter events, 370.3 us)
Async XLA Ops:
  7.2 83.7 %copy-start.59 = (bf16[1,4,2,128,768]{4,3,2,1,0:T(8,128)(2,1)S(1)}, bf16[1,4,2,128,768]{4,3,2,1,0:T(8,128)(2,1)}, u32[]{:S(2)}) copy-start(bf16[1,4,2,128,768]{4,3,2,1,0:T(8,128)(2,1)} %param.8) | copy-start | bytes 4718596
  7.2 106.8 %all-gather.5.cloned.1.call-start = ((), (), s32[]{:S(2)}) async-start(), calls=%async_computation.7 | async-start | bytes 3760128 | tf_op jit(solution)/shard_map/all_gather | solution.py:193
  7.9 112.3 %all-gather.7.cloned.1.call-start = ((), (), s32[]{:S(2)}) async-start(), calls=%async_computation.8 | async-start | bytes 1253376 | tf_op jit(solution)/shard_map/all_gather | solution.py:194
  8.7 147.8 %all-gather.9.cloned.1.call-start = ((), (), s32[]{:S(2)}) async-start(), calls=%async_computation.9 | async-start | bytes 5013504 | tf_op jit(solution)/shard_map/all_gather | solution.py:195
  9.4 201.2 %all-gather.11.cloned.1.call-start = ((), (), s32[]{:S(2)}) async-start(), calls=%async_computation.10 | async-start | bytes 5013504 | tf_op jit(solution)/shard_map/all_gather | solution.py:196
  10.0 673.0 %reduce-scatter.22.cloned.1.call-start = ((), (), s32[]{:S(2)}) async-start(), calls=%async_computation.15 | async-start | bytes 417792
  98.6 128.5 %copy-start.72 = (bf16[1,1,2,128,768]{4,3,2,1,0:T(8,128)(2,1)}, bf16[1,1,2,128,768]{4,3,2,1,0:T(8,128)(2,1)S(1)}, u32[]{:S(2)}) copy-start(bf16[1,1,2,128,768]{4,3,2,1,0:T(8,128)(2,1)S(1)} %get-tuple-element.109) | copy-start | bytes 1179652
  98.6 166.4 %copy-start.74 = (bf16[1,1,2,128,768]{4,3,2,1,0:T(8,128)(2,1)}, bf16[1,1,2,128,768]{4,3,2,1,0:T(8,128)(2,1)S(1)}, u32[]{:S(2)}) copy-start(bf16[1,1,2,128,768]{4,3,2,1,0:T(8,128)(2,1)S(1)} %get-tuple-element.107) | copy-start | bytes 1179652
  122.2 88.4 %copy-start.56 = (f32[256,768]{1,0:T(8,128)}, f32[256,768]{1,0:T(8,128)S(1)}, u32[]{:S(2)}) copy-start(f32[256,768]{1,0:T(8,128)S(1)} %get-tuple-element.138) | copy-start | bytes 2359300
  214.9 12.2 %collective-permute-start = (bf16[256,768]{1,0:T(8,128)(2,1)S(1)}, bf16[256,768]{1,0:T(8,128)(2,1)S(1)}, u32[]{:S(2)}, u32[]{:S(2)}) collective-permute-start(bf16[256,768]{1,0:T(8,128)(2,1)S(1)} %fusion.172), channel_id=1, source_target_pairs={{0,16},{1,17},{2,18},{3,19},{4,20},{5,21},{6,22},{7,23},{8,24},{9,... | collective-permute-start | bytes 1179656 | tf_op jit(solution)/shard_map/ppermute | solution.py:16
  252.5 12.5 %collective-permute-start.1 = (bf16[256,768]{1,0:T(8,128)(2,1)S(1)}, bf16[256,768]{1,0:T(8,128)(2,1)S(1)}, u32[]{:S(2)}, u32[]{:S(2)}) collective-permute-start(bf16[256,768]{1,0:T(8,128)(2,1)S(1)} %fusion.169), channel_id=1, source_target_pairs={{0,16},{1,17},{2,18},{3,19},{4,20},{5,21},{6,22},{7,23},{8,24},{9,... | collective-permute-start | bytes 1179656 | tf_op jit(solution)/shard_map/ppermute | solution.py:16
  287.4 11.6 %collective-permute-start.2 = (bf16[256,768]{1,0:T(8,128)(2,1)S(1)}, bf16[256,768]{1,0:T(8,128)(2,1)S(1)}, u32[]{:S(2)}, u32[]{:S(2)}) collective-permute-start(bf16[256,768]{1,0:T(8,128)(2,1)S(1)} %fusion.166), channel_id=1, source_target_pairs={{0,16},{1,17},{2,18},{3,19},{4,20},{5,21},{6,22},{7,23},{8,24},{9,... | collective-permute-start | bytes 1179656 | tf_op jit(solution)/shard_map/ppermute | solution.py:16
  299.2 140.6 %copy-start.21 = (bf16[256,768]{1,0:T(8,128)(2,1)}, bf16[256,768]{1,0:T(8,128)(2,1)S(1)}, u32[]{:S(2)}) copy-start(bf16[256,768]{1,0:T(8,128)(2,1)S(1)} %get-tuple-element.84) | copy-start | bytes 1179652
  322.1 10.6 collective-permute-start.3
  400.6 10.1 collective-permute-start.4
  440.3 9.9 collective-permute-start.5
  482.8 9.9 collective-permute-start.6
  521.6 9.9 collective-permute-start.7
  555.6 128.8 %reduce-scatter.26.cloned.1.call-start = ((), (), s32[]{:S(2)}) async-start(), calls=%async_computation.17 | async-start | bytes 1671168
  560.0 169.6 %reduce-scatter.24.cloned.1.call-start = ((), (), s32[]{:S(2)}) async-start(), calls=%async_computation.16 | async-start | bytes 417792
  563.9 232.6 %reduce-scatter.16.cloned.1.call-start = ((), (), s32[]{:S(2)}) async-start(), calls=%async_computation.12 | async-start | bytes 2506752 | tf_op jit(solution)/shard_map/reduce_scatter | solution.py:266
  570.0 320.2 %reduce-scatter.14.cloned.1.call-start = ((), (), s32[]{:S(2)}) async-start(), calls=%async_computation.11 | async-start | bytes 7520256 | tf_op jit(solution)/shard_map/reduce_scatter | solution.py:265
  593.5 412.6 %reduce-scatter.18.cloned.1.call-start = ((), (), s32[]{:S(2)}) async-start(), calls=%async_computation.13 | async-start | bytes 10027008 | tf_op jit(solution)/shard_map/reduce_scatter | solution.py:267
  635.0 486.9 %reduce-scatter.20.cloned.1.call-start = ((), (), s32[]{:S(2)}) async-start(), calls=%async_computation.14 | async-start | bytes 10027008 | tf_op jit(solution)/shard_map/reduce_scatter | solution.py:268
  (353 other events, 1919.8 us)
Sparse Core Ops, SparseCore 0:
  10.3 52.3 all-gather.4
  65.0 36.7 all-gather.6
  104.1 52.3 all-gather.8
  158.6 51.9 all-gather.10
  555.7 53.2 reduce-scatter.21
  613.0 58.5 reduce-scatter.25
  675.0 54.5 reduce-scatter.23
  734.4 62.0 reduce-scatter.15
  801.0 89.1 reduce-scatter.13
  895.3 110.8 reduce-scatter.17
  1010.8 111.0 reduce-scatter.19
where the time goes:
time: 1140 us; the launch traced here: 1130 us
  waiting for transfers between devices  564 us (49%)
  matrix products  293 us (26%)
  local copies, waits for them, and re-layouts  121 us (11%)
  blocking collectives  75 us (7%)
  other arithmetic  30 us (3%)
  starting transfers between devices  25.8 us (2%)
  between operations  20 us (2%)
    reduce_scatter x1, waiting for transfers between devices, body(): lax.psum_scatter(totals[2][None], 'fsdp', scatter_dimension=1, tiled=True)  116 us
    reduce_scatter x1, waiting for transfers between devices, body(): lax.psum_scatter(totals[3][None], 'fsdp', scatter_dimension=1, tiled=True)  116 us
    reduce_scatter x1, waiting for transfers between devices, body(): lax.psum_scatter(totals[0][None], 'fsdp', scatter_dimension=1, tiled=True)  93.7 us
    reduce_scatter x1, waiting for transfers between devices, body(): lax.psum_scatter(totals[1][None], 'fsdp', scatter_dimension=1, tiled=True)  65.3 us
    dot_general x5, matrix products, layer_forward(): jnp.dot(normed_two, up_weight, preferred_element_type=jnp.float32)  56.5 us
    ppermute x8, waiting for transfers between devices, from_behind(): return lax.ppermute(block, axis, route)  50.4 us
    unnamed x14, waiting for transfers between devices  46.4 us
    all_gather x1, waiting for transfers between devices, body(): lax.all_gather(shards[3], 'fsdp', axis=1, tiled=True)  42.3 us
  transfers between devices with their start and end apart: 19, of which 15 were waited for; matrix products, arithmetic and copies ran while one was open for 16% of the time, Pallas kernels for 0%

commit v1 on v0

--- a/solution.py
+++ b/solution.py
@@ -1,13 +1,888 @@
+import functools
+import math
+
 import jax
 import jax.numpy as jnp
 from jax import lax
+from jax.experimental import pallas as pl
+from jax.experimental.pallas import tpu as pltpu
 from jax.sharding import PartitionSpec as P
+
+MESH = pl.DeviceIdType.MESH
 
 HEADS = 12
 HEAD_DIM = 64
-
-
 epsilon = 1e-05
+BF, F32 = jnp.bfloat16, jnp.float32
+NT = (((1,), (1,)), ((), ()))
+TN = (((0,), (0,)), ((), ()))
+
+SIDE, ACROSS, UP, DOWN = range(4)
+LEVELS_FIRST, ACROSS_FIRST = 0, 1
+
+class Sends:
+    def __init__(self):
+        self.items = []
+
+    def start(self, copy, when):
+        if when is None:
+            copy.start()
+        else:
+            pl.when(when)(copy.start)
+        self.items.append((copy, when))
+
+    def drain(self):
+        for copy, when in self.items:
+            if when is None:
+                copy.wait_send()
+            else:
+                pl.when(when)(copy.wait_send)
+
+
+def matmul(left, right, dims=(((1,), (0,)), ((), ()))):
+    return lax.dot_general(left, right, dims, preferred_element_type=F32)
+
+
+def standard(features):
+    centred = features - jnp.mean(features, axis=-1, keepdims=True)
+    scale = lax.rsqrt(jnp.mean(centred * centred, axis=-1, keepdims=True) + epsilon)
+    return centred * scale, scale
+
+
+def gelu_and_slope(raised):
+    share = 0.5 + 0.5 * lax.erf(raised * math.sqrt(0.5))
+    bell = jnp.exp(raised * raised * -0.5) * (1.0 / math.sqrt(2.0 * math.pi))
+    return raised * share, share + raised * bell
+
+
+def norm_back(upper, normal, scale):
+    shift = jnp.mean(upper, axis=-1, keepdims=True)
+    slope = jnp.mean(upper * normal, axis=-1, keepdims=True)
+    return (upper - shift - normal * slope) * scale
+
+
+def column_sum(values):
+    return jnp.sum(values, axis=0, keepdims=True)
+
+
+def pair_parts(matrix):
+    lane = lax.broadcasted_iota(jnp.int32, matrix.shape, 1)
+    zero = jnp.zeros_like(matrix)
+    first = lane < HEAD_DIM
+    return jnp.concatenate([jnp.where(first, matrix, zero), jnp.where(first, zero, matrix)], axis=0)
+
+
+def pair_join(stacked):
+    rows = stacked.shape[0] // 2
+    lane = lax.broadcasted_iota(jnp.int32, (rows, stacked.shape[1]), 1)
+    return jnp.where(lane < HEAD_DIM, stacked[:rows], stacked[rows:])
+
+
+def halves(scores):
+    keys = scores.shape[1] // 2
+    return scores[:, :keys], scores[:, keys:]
+
+
+class Place:
+    def __init__(self, levels):
+        self.levels = levels
+        self.section, self.mine = lax.axis_index("section"), lax.axis_index("fsdp")
+        self.level = lax.div(self.mine, 4)
+        self.row = lax.rem(lax.div(self.mine, 2), 2)
+        self.core = lax.rem(self.mine, 2)
+        self.has_up, self.has_down = self.level < levels - 1, self.level > 0
+        self.targets = {SIDE: self.mine ^ 1, ACROSS: self.mine ^ 2, UP: self.mine + 4, DOWN: self.mine - 4}
+
+    def block(self, level, row, core):
+        return level * 4 + row * 2 + core
+
+    def greet(self):
+        barrier = pltpu.get_barrier_semaphore()
+
+        def hello(section, target):
+            pl.semaphore_signal(barrier, inc=1, device_id=(section, target), device_id_type=MESH)
+
+        hello(1 - self.section, self.mine)
+        hello(self.section, self.targets[SIDE])
+        hello(self.section, self.targets[ACROSS])
+        pl.when(self.has_down)(lambda: hello(self.section, self.targets[DOWN]))
+        pl.when(self.has_up)(lambda: hello(self.section, self.targets[UP]))
+        ends = (self.level == 0).astype(jnp.int32) + (self.level == self.levels - 1).astype(jnp.int32)
+        pl.semaphore_wait(barrier, 5 - ends)
+
+
+class Gather:
+    def __init__(self, place, shards, wholes, kinds, send_sem, recv_sem, local_sem):
+        self.place, self.shards, self.wholes, self.kinds = place, shards, wholes, kinds
+        self.send_sem, self.recv_sem, self.local_sem = send_sem, recv_sem, local_sem
+        self.sends, self.local = Sends(), []
+
+    def send(self, piece, block, way, own=False, when=None):
+        target = self.wholes[piece](block)
+        copy = pltpu.make_async_remote_copy(
+            src_ref=self.shards[piece] if own else target,
+            dst_ref=target,
+            send_sem=self.send_sem.at[piece, block, way],
+            recv_sem=self.recv_sem.at[piece, block],
+            device_id=(self.place.section, self.place.targets[way]),
+            device_id_type=MESH,
+        )
+        self.sends.start(copy, when)
+
+    def arrived(self, piece, block, when=None):
+        target = self.wholes[piece](block)
+        copy = pltpu.make_async_remote_copy(
+            src_ref=target,
+            dst_ref=target,
+            send_sem=self.send_sem.at[piece, block, 0],
+            recv_sem=self.recv_sem.at[piece, block],
+            device_id=(self.place.section, self.place.targets[SIDE]),
+            device_id_type=MESH,
+        )
+        if when is None:
+            copy.wait_recv()
+        else:
+            pl.when(when)(copy.wait_recv)
+
+    def start(self):
+        mine = self.place.mine
+        for piece in range(len(self.shards)):
+            self.send(piece, mine, ACROSS, own=True)
+            self.send(piece, mine, UP, own=True, when=self.place.has_up)
+            self.send(piece, mine, DOWN, own=True, when=self.place.has_down)
+            self.send(piece, mine, SIDE, own=True)
+            copy = pltpu.make_async_copy(
+                self.shards[piece], self.wholes[piece](mine), self.local_sem.at[piece]
+            )
+            copy.start()
+            self.local.append(copy)
+
+    def first_across(self, piece):
+        block = self.place.mine ^ 2
+        self.arrived(piece, block)
+        self.send(piece, block, UP, when=self.place.has_up)
+        self.send(piece, block, DOWN, when=self.place.has_down)
+        self.send(piece, block, SIDE)
+
+    def from_levels(self, piece, distance):
+        place = self.place
+        plain = self.kinds[piece] == "level"
+        for row in (place.row,) if plain else (place.row, 1 - place.row):
+            for sign in (-1, 1):
+                other = place.level + sign * distance
+                here = other >= 0 if sign < 0 else other < place.levels
+                onward = place.has_up if sign < 0 else place.has_down
+                block = place.block(other, row, place.core)
+                self.arrived(piece, block, here)
+                if distance < place.levels - 1:
+                    self.send(piece, block, UP if sign < 0 else DOWN, when=jnp.logical_and(here, onward))
+                if plain:
+                    self.send(piece, block, ACROSS, when=here)
+                self.send(piece, block, SIDE, when=here)
+
+    def from_across(self, piece, distance):
+        place = self.place
+        if self.kinds[piece] != "level":
+            return
+        for sign in (-1, 1) if distance else (1,):
+            other = place.level + sign * distance
+            here = None
+            if distance:
+                here = other >= 0 if sign < 0 else other < place.levels
+            block = place.block(other, 1 - place.row, place.core)
+            self.arrived(piece, block, here)
+            self.send(piece, block, SIDE, when=here)
+
+    def from_side(self, piece):
+        for level in range(self.place.levels):
+            for row in range(2):
+                self.arrived(piece, self.place.block(level, row, 1 - self.place.core))
+
+    def drain(self):
+        for copy in self.local:
+            copy.wait()
+        self.sends.drain()
+
+
+class Chunk:
+    def __init__(self, place, order, part, start, refs, sems):
+        self.place, self.order, self.levels = place, order, place.levels
+        self.whole, self.start = part, start
+        self.from_side, self.from_across, self.from_chain = refs
+        self.cols = self.from_side.shape[2]
+        (
+            self.side_out,
+            self.side_in,
+            self.across_out,
+            self.across_in,
+            self.up_out,
+            self.down_out,
+            self.chain_in,
+        ) = sems
+
+    def part(self, block):
+        return self.whole.at[block, :, pl.ds(self.start, self.cols)]
+
+    def copy(self, block, target, out_sem, in_sem, way):
+        return pltpu.make_async_remote_copy(
+            src_ref=self.part(block),
+            dst_ref=target,
+            send_sem=out_sem,
+            recv_sem=in_sem,
+            device_id=(self.place.section, self.place.targets[way]),
+            device_id_type=MESH,
+        )
+
+    def side(self, pair):
+        block = pair * 2 + 1 - self.place.core
+        return self.copy(
+            block, self.from_side.at[pair], self.side_out.at[pair], self.side_in.at[pair], SIDE
+        )
+
+    def across(self, level, slot):
+        block = self.place.block(level, 1 - self.place.row, self.place.core)
+        return self.copy(
+            block,
+            self.from_across.at[slot],
+            self.across_out.at[slot],
+            self.across_in.at[slot],
+            ACROSS,
+        )
+
+    def below_index(self, target, level):
+        return target - level
+
+    def above_index(self, target):
+        return self.levels - target
+
+    def up(self, row, slot, target):
+        index = self.below_index(target, self.place.level + 1)
+        return self.copy(
+            self.place.block(target, row, self.place.core),
+            self.from_chain.at[slot, index],
+            self.up_out.at[slot, target],
+            self.chain_in.at[slot, index],
+            UP,
+        )
+
+    def down(self, row, slot, target):
+        index = self.above_index(target)
+        return self.copy(
+            self.place.block(target, row, self.place.core),
+            self.from_chain.at[slot, index],
+            self.down_out.at[slot, target],
+            self.chain_in.at[slot, index],
+            DOWN,
+        )
+
+    def arrived(self, slot, index):
+        target = self.from_chain.at[slot, index]
+        pltpu.make_async_remote_copy(
+            src_ref=target,
+            dst_ref=target,
+            send_sem=self.side_out.at[0],
+            recv_sem=self.chain_in.at[slot, index],
+            device_id=(self.place.section, self.place.targets[SIDE]),
+            device_id_type=MESH,
+        ).wait_recv()
+
+    def add(self, block, term):
+        part = self.part(block)
+        total = part[...].astype(F32) + term.astype(F32)
+        part[...] = total.astype(part.dtype)
+
+    def send_side(self):
+        @pl.loop(0, self.levels * 2)
+        def _(pair):
+            self.side(pair).start()
+
+    def join_side(self):
+        place = self.place
+        for other in (True, False):
+            row = 1 - place.row if other else place.row
+
+            @pl.loop(0, self.levels)
+            def _(level):
+                pair = level * 2 + row
+                self.side(pair).wait_recv()
+                self.add(pair * 2 + place.core, self.from_side[pair])
+                if other and self.order == ACROSS_FIRST:
+                    self.across(level, level).start()
+
+    def join_across(self):
+        place = self.place
+
+        @pl.loop(0, self.levels)
+        def _(level):
+            self.across(level, level).wait_recv()
+            self.add(place.block(level, place.row, place.core), self.from_across[level])
+
+    def rows(self):
+        row = self.place.row
+        return ((0, row), (1, 1 - row)) if self.order == LEVELS_FIRST else ((0, row),)
+
+    def chain_start(self):
+        level, last = self.place.level, self.levels - 1
+        for slot, row in self.rows():
+            for target in range(self.levels):
+                if target:
+                    pl.when(level == 0)(self.up(row, slot, self.levels - target).start)
+                    pl.when(level == last)(self.down(row, slot, target - 1).start)
+
+    def chain_pass(self, distance):
+        place, last = self.place, self.levels - 1
+        for slot, row in self.rows():
+            for target in range(last, distance, -1):
+
+                @pl.when(place.level == distance)
+                def _():
+                    index = self.below_index(target, place.level)
+                    self.arrived(slot, index)
+                    self.add(place.block(target, row, place.core), self.from_chain[slot, index])
+                    self.up(row, slot, target).start()
+
+            for target in range(last - distance):
+
+                @pl.when(place.level == last - distance)
+                def _():
+                    index = self.above_index(target)
+                    self.arrived(slot, index)
+                    self.add(place.block(target, row, place.core), self.from_chain[slot, index])
+                    self.down(row, slot, target).start()
+
+    def chain_end(self, out):
+        place, last = self.place, self.levels - 1
+        for slot, row in reversed(self.rows()):
+            block = place.block(place.level, row, place.core)
+
+            @pl.when(place.level > 0)
+            def _():
+                index = self.below_index(place.level, place.level)
+                self.arrived(slot, index)
+                self.add(block, self.from_chain[slot, index])
+
+            @pl.when(place.level < last)
+            def _():
+                index = self.above_index(place.level)
+                self.arrived(slot, index)
+                self.add(block, self.from_chain[slot, index])
+
+            if slot == 1:
+                self.across(place.level, 0).start()
+        if self.order == ACROSS_FIRST:
+            out(self.part(place.mine)[...].astype(F32))
+
+    def finish(self, out):
+        if self.order == LEVELS_FIRST:
+            self.across(self.place.level, 0).wait_recv()
+            out(self.part(self.place.mine)[...].astype(F32) + self.from_across[0].astype(F32))
+
+    def drain(self):
+        @pl.loop(0, self.levels * 2)
+        def _(pair):
+            self.side(pair).wait_send()
+
+        if self.order == ACROSS_FIRST:
+
+            @pl.loop(0, self.levels)
+            def _(level):
+                self.across(level, level).wait_send()
+
+        else:
+            self.across(self.place.level, 0).wait_send()
+        for slot, row in self.rows():
+            for target in range(self.levels):
+                pl.when(self.place.level < target)(self.up(row, slot, target).wait_send)
+                pl.when(self.place.level > target)(self.down(row, slot, target).wait_send)
+
+
+def chunk_scratch(levels, order, rows, cols, dtype, shared):
+    block = (rows, cols)
+    slots = 2 if order == LEVELS_FIRST else 1
+    crossing = 1 if order == LEVELS_FIRST else levels
+    dma = pltpu.SemaphoreType.DMA
+    from_side = [] if shared else [pltpu.VMEM((levels * 2,) + block, dtype)]
+    return from_side + [
+        pltpu.VMEM((crossing,) + block, dtype),
+        pltpu.VMEM((slots, levels + 1) + block, dtype),
+        dma((levels * 2,)),
+        dma((levels * 2,)),
+        dma((crossing,)),
+        dma((crossing,)),
+        dma((slots, levels)),
+        dma((slots, levels)),
+        dma((slots, levels + 1)),
+    ]
+
+
+CHUNK_REFS = 9
+
+
+def pad_lanes(rows, lanes=128):
+    missing = lanes - rows.shape[1]
+    if not missing:
+        return rows
+    return jnp.concatenate([rows, jnp.zeros((rows.shape[0], missing), rows.dtype)], axis=1)
+
+
+def tile_of(rows):
+    missing = 8 - rows.shape[0]
+    if not missing:
+        return rows
+    return jnp.concatenate([rows, jnp.zeros((missing, rows.shape[1]), rows.dtype)], axis=0)
+
+
+def fold(line):
+    pieces = [pad_lanes(line[:, at : at + 128]) for at in range(0, line.shape[1], 128)]
+    return tile_of(jnp.concatenate(pieces, axis=0))
+
+
+def unfold(rows, count):
+    pieces = []
+    for index in range(-(-count // 128)):
+        pieces.append(rows[index : index + 1, : min(128, count - index * 128)])
+    return jnp.concatenate(pieces, axis=1)
+
+
+def relay_kernel(levels, clips, plan, *refs):
+    own, attend_shard, merge_shard, up_shard, down_shard, gain_shard, shift_shard, bias_shard = refs[:8]
+    out, gain_out, shift_out, attend_out, merge_out, up_out, bias_out, down_out = refs[8:16]
+    (
+        packed,
+        vector_blocks,
+        attend_blocks,
+        merge_blocks,
+        up_blocks,
+        down_blocks,
+        vectors,
+        bias,
+        vector_sum,
+        bias_sum,
+        entry,
+        projected,
+        probability,
+        normed,
+        attended,
+        middle,
+        normed_two,
+        activated,
+        slope,
+        leaving,
+        low_temp,
+        temp,
+        sum_temp,
+        gather_send,
+        gather_recv,
+        gather_local,
+        load_sem,
+        send_sem,
+        recv_sem,
+        out_sem,
+        free_sem,
+    ) = refs[16:47]
+    chunk_refs = list(refs[47:])
+    place = Place(levels)
+    section, mine = place.section, place.mine
+    batches, rows, width = own.shape
+    wide = up_shard.shape[1]
+    ways = levels * 4
+    share, wide_share = width // ways, wide // ways
+    length = rows // clips
+    pairs = HEADS // 2
+    total = batches * rows
+
+    load_own = pltpu.make_async_copy(own, entry.at[0], load_sem)
+    load_own.start()
+    packed[0:8] = pad_lanes(
+        jnp.concatenate([gain_shard[...], shift_shard[...]], axis=0).astype(F32)
+    )
+    packed[8:16] = fold(bias_shard[...].astype(F32))
+    place.greet()
+
+    half_share = wide_share // 2
+    shards = [
+        packed,
+        attend_shard,
+        up_shard,
+        merge_shard,
+        down_shard.at[pl.ds(0, half_share)],
+        down_shard.at[pl.ds(half_share, half_share)],
+    ]
+    wholes = [
+        lambda block: vector_blocks.at[block],
+        lambda block: attend_blocks.at[block],
+        lambda block: up_blocks.at[block],
+        lambda block: merge_blocks.at[block],
+        lambda block: down_blocks.at[block, pl.ds(0, half_share)],
+        lambda block: down_blocks.at[block, pl.ds(half_share, half_share)],
+    ]
+    kinds = ["level"] * 5 + ["across"]
+    gather = Gather(place, shards, wholes, kinds, gather_send, gather_recv, gather_local)
+    count = len(shards)
+    gather.start()
+    gather.first_across(count - 1)
+    for distance in range(1, levels):
+        for piece in range(count):
+            gather.from_levels(piece, distance)
+            gather.from_across(piece, distance - 1)
+    for piece in range(count):
+        gather.from_across(piece, levels - 1)
+    for piece in range(count):
+        gather.from_side(piece)
+    gather.drain()
+    vectors[...] = jnp.concatenate([vector_blocks[block, 0:8, 0:share] for block in range(ways)], axis=1)
+    bias[...] = jnp.concatenate(
+        [unfold(vector_blocks[block, 8:16], wide_share) for block in range(ways)], axis=1
+    )
+
+    def flat(blocks):
+        return blocks.reshape(-1, blocks.shape[-1])
+
+    def relay(batch):
+        return pltpu.make_async_remote_copy(
+            src_ref=leaving.at[batch],
+            dst_ref=entry.at[1, batch],
+            send_sem=send_sem.at[batch],
+            recv_sem=recv_sem.at[batch],
+            device_id=(1 - section, mine),
+            device_id_type=MESH,
+        )
+
+    def keep(batch):
+        return pltpu.make_async_copy(leaving.at[batch], out.at[batch], out_sem.at[batch])
+
+    vector_sum[...] = jnp.zeros_like(vector_sum)
+    bias_sum[...] = jnp.zeros_like(bias_sum)
+    fed, back = section, 1 - section
+
+    def row(index):
+        return vectors[index : index + 1, :]
+
+    def chances(batch, index):
+        at = pl.multiple_of(batch * 4 * length + (index % 2) * 2 * length, 128)
+        return probability.at[pl.ds((index // 2) * length, length), pl.ds(at, 2 * length)]
+
+    def forward(batch):
+        normal, _ = standard(entry[fed, batch].astype(F32))
+        normed[batch] = (normal * row(0) + row(2)).astype(BF)
+        for part, shift in ((0, 4), (1, None), (2, 5)):
+            at = slice(part * width, (part + 1) * width)
+            value = matmul(normed[batch], flat(attend_blocks[:, :, at]))
+            if shift is not None:
+                value = value + row(shift)
+            projected[batch, :, at] = value.astype(BF)
+        for clip in range(clips):
+            span = slice(clip * length, (clip + 1) * length)
+            for pair in range(pairs):
+                lanes = [slice(p * width + pair * 128, p * width + pair * 128 + 128) for p in range(3)]
+                query = projected[batch, span, lanes[0]] * jnp.asarray(HEAD_DIM**-0.5, BF)
+                key = pair_parts(projected[batch, span, lanes[1]])
+                scores = matmul(query, key, NT)
+                parts = []
+                for half in halves(scores):
+                    exponent = jnp.exp(half - jnp.max(half, axis=-1, keepdims=True))
+                    parts.append(exponent * (1.0 / jnp.sum(exponent, axis=-1, keepdims=True)))
+                weight = jnp.concatenate(parts, axis=1).astype(BF)
+                chances(batch, clip * pairs + pair)[...] = weight
+                value = pair_parts(projected[batch, span, lanes[2]])
+                attended[batch, span, lanes[0]] = matmul(weight, value).astype(BF)
+        joined = matmul(attended[batch], flat(merge_blocks[...])) + row(6)
+        temp[...] = entry[fed, batch].astype(F32) + joined
+        middle[batch] = temp[...].astype(BF)
+        normal, _ = standard(temp[...])
+        normed_two[batch] = (normal * row(1) + row(3)).astype(BF)
+        tile = 256
+        for start in range(0, wide, tile):
+            at = slice(start, start + tile)
+            value, rate = gelu_and_slope(
+                matmul(normed_two[batch], flat(up_blocks[:, :, at])) + bias[:, at]
+            )
+            activated[batch, :, at] = value.astype(BF)
+            slope[batch, :, at] = rate.astype(BF)
+        result = temp[...] + matmul(activated[batch], flat(down_blocks[...])) + row(7)
+        leaving[batch] = result.astype(BF)
+
+    def backward(batch):
+        low = entry[back, batch]
+        vector_sum[7:8] += column_sum(low.astype(F32))
+        blocks = 4
+        for block in range(0, ways, blocks):
+            at = slice(block * wide_share, (block + blocks) * wide_share)
+            rate = matmul(low, flat(down_blocks[block : block + blocks]), NT)
+            rate = rate * slope[batch, :, at].astype(F32)
+            bias_sum[:, at] += column_sum(rate)
+            slope[batch, :, at] = rate.astype(BF)
+        temp[...] = matmul(slope[batch], flat(up_blocks[...]), NT)
+        normal, scale = standard(middle[batch].astype(F32))
+        grad = temp[...]
+        vector_sum[1:2] += column_sum(grad * normal)
+        vector_sum[3:4] += column_sum(grad)
+        grad = entry[back, batch].astype(F32) + norm_back(grad * row(1), normal, scale)
+        sum_temp[...] = grad
+        vector_sum[6:7] += column_sum(grad)
+        middle[batch] = grad.astype(BF)
+        low_temp[...] = matmul(middle[batch], flat(merge_blocks[...]), NT).astype(BF)
+        for clip in range(clips):
+            span = slice(clip * length, (clip + 1) * length)
+            for pair in range(pairs):
+                lanes = [slice(p * width + pair * 128, p * width + pair * 128 + 128) for p in range(3)]
+                query = projected[batch, span, lanes[0]]
+                key = pair_parts(projected[batch, span, lanes[1]])
+                value = pair_parts(projected[batch, span, lanes[2]])
+                upper = low_temp[span, lanes[0]]
+                weight = chances(batch, clip * pairs + pair)[...]
+                rise = matmul(upper, value, NT)
+                value_grad = pair_join(matmul(weight, upper, TN))
+                parts = []
+                for part, heavy in zip(halves(rise), halves(weight)):
+                    heavy = heavy.astype(F32)
+                    mean = jnp.sum(part * heavy, axis=-1, keepdims=True)
+                    parts.append(heavy * (part - mean) * HEAD_DIM**-0.5)
+                change = jnp.concatenate(parts, axis=1).astype(BF)
+                query_grad = matmul(change, key)
+                key_grad = pair_join(matmul(change, query, TN))
+                vector_sum[4:5, lanes[0]] += column_sum(query_grad)
+                vector_sum[5:6, lanes[0]] += column_sum(value_grad)
+                for at, piece in zip(lanes, (query_grad, key_grad, value_grad)):
+                    projected[batch, span, at] = piece.astype(BF)
+        temp[...] = matmul(projected[batch], flat(attend_blocks[...]), NT)
+        normal, scale = standard(entry[fed, batch].astype(F32))
+        grad = temp[...]
+        vector_sum[0:1] += column_sum(grad * normal)
+        vector_sum[2:3] += column_sum(grad)
+        leaving[batch] = (sum_temp[...] + norm_back(grad * row(0), normal, scale)).astype(BF)
+
+    load_own.wait()
+
+    @pl.loop(0, 2 * batches)
+    def _(step):
+        is_forward = jnp.where(section == 0, step < batches, lax.rem(step, 2) == 0)
+        batch = jnp.where(section == 0, lax.rem(step, batches), lax.div(step, 2))
+
+        @pl.when(is_forward)
+        def _():
+            pl.when(section == 1)(relay(batch).wait_recv)
+            forward(batch)
+            pl.when(section == 0)(relay(batch).start)
+            pl.when(section == 1)(keep(batch).start)
+
+        @pl.when(jnp.logical_not(is_forward))
+        def _():
+            pl.when(section == 0)(relay(batch).wait)
+            pl.when(section == 1)(keep(batch).wait)
+            backward(batch)
+            pl.when(section == 1)(relay(batch).start)
+            pl.when(section == 0)(keep(batch).start)
+
+    chunks = []
+    part_refs = [vector_blocks, attend_blocks, merge_blocks, up_blocks, down_blocks]
+    for which, start, order, _, cols, _, shared in plan:
+        if shared is None:
+            from_side = chunk_refs.pop(0)
+        else:
+            from_side = chunks[shared].from_side.at[:, :, pl.ds(0, cols)]
+        held, chunk_refs = chunk_refs[:CHUNK_REFS], chunk_refs[CHUNK_REFS:]
+        chunks.append(Chunk(place, order, part_refs[which], start, [from_side] + held[:2], held[2:]))
+    down_a, down_b, up_a, up_b, attend_a, attend_b, merge, vector = chunks
+
+    def store(target, chunk):
+        def put(value):
+            target[:, pl.ds(chunk.start, chunk.cols)] = value
+
+        return put
+
+    def turn(source, place_at):
+        target = probability.at[pl.ds(0, width), pl.ds(place_at * total, total)]
+        target[...] = flat(source[...]).T
+        return target
+
+    def columns(left, source, chunk, credit=None):
+        step = 128 * max(d for d in (1, 2, 3) if chunk.cols % (128 * d) == 0)
+
+        @pl.loop(0, chunk.cols // step)
+        def _(index):
+            at = pl.multiple_of(chunk.start + index * step, 128)
+            product = matmul(left[...], flat(source[:, :, pl.ds(at, step)]))
+            chunk.whole[:, :, pl.ds(at, step)] = product.astype(BF).reshape(ways, width // ways, step)
+
+        if credit is not None:
+            pl.semaphore_wait(free_sem.at[credit], 1)
+        chunk.send_side()
+
+    def release(index):
+        pl.semaphore_signal(
+            free_sem.at[index], inc=1, device_id=(section, place.targets[SIDE]), device_id_type=MESH
+        )
+
+    pair_cols = 2 * wide_share
+
+    @pl.loop(0, levels * 2)
+    def _(pair):
+        tile = flat(activated[:, :, pl.ds(pl.multiple_of(pair * pair_cols, 128), pair_cols)])
+        for chunk in (down_a, down_b):
+            at = pl.ds(chunk.start, chunk.cols)
+            product = matmul(tile, flat(entry[back, :, :, at]), TN).astype(BF)
+            for core in range(2):
+                down_blocks[pair * 2 + core, :, at] = product[core * wide_share : (core + 1) * wide_share]
+            chunk.side(pair).start()
+
+    for block in range(ways):
+        vector_blocks[block, 0:8] = pad_lanes(vector_sum[:, block * share : (block + 1) * share])
+        vector_blocks[block, 8:16] = fold(bias_sum[:, block * wide_share : (block + 1) * wide_share])
+    vector.send_side()
+    down_a.join_side()
+    down_a.chain_start()
+    down_b.join_side()
+    vector.join_side()
+    turned = turn(normed_two, 0)
+    columns(turned, slope, up_a)
+    columns(turned, slope, up_b)
+    up_a.join_side()
+    release(0)
+    down_a.chain_pass(1)
+    up_b.join_side()
+    release(1)
+    turned = turn(normed, 1)
+    columns(turned, projected, attend_a, 0)
+    down_a.chain_pass(2)
+    down_b.join_across()
+    down_b.chain_start()
+    vector.join_across()
+    vector.chain_start()
+    columns(turned, projected, attend_b, 1)
+    attend_a.join_side()
+    turned = turn(attended, 0)
+    columns(turned, middle, merge)
+    attend_b.join_side()
+    down_b.chain_pass(1)
+    merge.join_side()
+    down_a.chain_end(None)
+    up_a.join_across()
+    up_a.chain_start()
+    down_b.chain_pass(2)
+    vector.chain_pass(1)
+    up_a.chain_pass(1)
+    up_b.join_across()
+    up_b.chain_start()
+    vector.chain_pass(2)
+    down_b.chain_end(store(down_out, down_b))
+    up_a.chain_pass(2)
+    up_b.chain_pass(1)
+    attend_a.join_across()
+    attend_a.chain_start()
+
+    def store_vectors(value):
+        gain_out[...] = value[0:2, :share]
+        shift_out[...] = value[2:8, :share]
+        bias_out[...] = unfold(value[8:16], wide_share)
+
+    vector.chain_end(store_vectors)
+    up_a.chain_end(store(up_out, up_a))
+    up_b.chain_pass(2)
+    attend_a.chain_pass(1)
+    attend_b.join_across()
+    attend_b.chain_start()
+    up_b.chain_end(store(up_out, up_b))
+    attend_a.chain_pass(2)
+    attend_b.chain_pass(1)
+    merge.join_across()
+    merge.chain_start()
+    attend_a.chain_end(store(attend_out, attend_a))
+    attend_b.chain_pass(2)
+    merge.chain_pass(1)
+    attend_b.chain_end(store(attend_out, attend_b))
+    merge.chain_pass(2)
+    down_a.finish(store(down_out, down_a))
+    merge.chain_end(store(merge_out, merge))
+    for chunk in chunks:
+        chunk.drain()
+
+    @pl.loop(0, batches)
+    def _(batch):
+        pl.when(section == 1)(relay(batch).wait_send)
+        pl.when(section == 0)(keep(batch).wait)
+
+
+def train_step(own, attend, merge, up, down, gains, shifts, bias, clips, ways, collective_id):
+    levels = ways // 4
+    batches, rows, width = own.shape
+    wide = up.shape[1]
+    share, wide_share = width // ways, wide // ways
+    length = rows // clips
+    plan = [
+        (4, 0, LEVELS_FIRST, wide_share, width // 2, BF, None),
+        (4, width // 2, ACROSS_FIRST, wide_share, width // 2, BF, None),
+        (3, 0, ACROSS_FIRST, share, wide // 2, BF, None),
+        (3, wide // 2, ACROSS_FIRST, share, wide // 2, BF, None),
+        (1, 0, ACROSS_FIRST, share, 3 * width // 2, BF, 2),
+        (1, 3 * width // 2, ACROSS_FIRST, share, 3 * width // 2, BF, 3),
+        (2, 0, ACROSS_FIRST, share, width, BF, None),
+        (0, 0, ACROSS_FIRST, 16, 128, F32, None),
+    ]
+    dma = pltpu.SemaphoreType.DMA
+    vmem, anywhere = pl.BlockSpec(memory_space=pltpu.VMEM), pl.BlockSpec(memory_space=pl.ANY)
+
+    def held(cols, dtype=BF):
+        return pltpu.VMEM((batches, rows, cols), dtype)
+
+    scratch = [
+        pltpu.VMEM((16, 128), F32),
+        pltpu.VMEM((ways, 16, 128), F32),
+        pltpu.VMEM((ways, share, 3 * width), BF),
+        pltpu.VMEM((ways, share, width), BF),
+        pltpu.VMEM((ways, share, wide), BF),
+        pltpu.VMEM((ways, wide_share, width), BF),
+        pltpu.VMEM((8, width), F32),
+        pltpu.VMEM((1, wide), F32),
+        pltpu.VMEM((8, width), F32),
+        pltpu.VMEM((1, wide), F32),
+        pltpu.VMEM((2, batches, rows, width), BF),
+        held(3 * width),
+        pltpu.VMEM((clips * HEADS // 4 * length, batches * 4 * length), BF),
+        held(width),
+        held(width),
+        held(width),
+        held(width),
+        held(wide),
+        held(wide),
+        held(width),
+        pltpu.VMEM((rows, width), BF),
+        pltpu.VMEM((rows, width), F32),
+        pltpu.VMEM((rows, width), F32),
+        dma((6, ways, 4)),
+        dma((6, ways)),
+        dma((6,)),
+        dma(()),
+        dma((batches,)),
+        dma((batches,)),
+        dma((batches,)),
+        pltpu.SemaphoreType.REGULAR((2,)),
+    ]
+    for _, _, order, chunk_rows, cols, dtype, shared in plan:
+        scratch += chunk_scratch(levels, order, chunk_rows, cols, dtype, shared is not None)
+
+    def grad(*shape):
+        return jax.ShapeDtypeStruct(shape, F32)
+
+    return pl.pallas_call(
+        functools.partial(relay_kernel, levels, clips, plan),
+        out_shape=[
+            jax.ShapeDtypeStruct(own.shape, BF),
+            grad(2, share),
+            grad(6, share),
+            grad(share, 3 * width),
+            grad(share, width),
+            grad(share, wide),
+            grad(1, wide_share),
+            grad(wide_share, width),
+        ],
+        in_specs=[anywhere] * 5 + [vmem] * 3,
+        out_specs=[anywhere] + [vmem] * 7,
+        scratch_shapes=scratch,
+        compiler_params=pltpu.CompilerParams(
+            collective_id=collective_id, has_side_effects=True, vmem_limit_bytes=63 * 2**20
+        ),
+    )(own, attend, merge, up, down, gains, shifts, bias)
 
 
 def from_behind(block, axis, distance):
@@ -178,7 +1053,7 @@
     )
 
 
-def body(
+def plain_body(
     section_inputs,
     norm_gains,
     offsets,
@@ -282,6 +1157,56 @@
     )
 
 
+def body(
+    section_inputs,
+    norm_gains,
+    offsets,
+    attend_weight,
+    merge_weight,
+    up_weight,
+    up_bias,
+    down_weight,
+):
+    ways = lax.axis_size("fsdp")
+    if ways % 4 or attend_weight.shape[1] % 16:
+        return plain_body(
+            section_inputs,
+            norm_gains,
+            offsets,
+            attend_weight,
+            merge_weight,
+            up_weight,
+            up_bias,
+            down_weight,
+        )
+    batches, clips, length, width = section_inputs.shape[1:]
+    own = section_inputs.reshape(batches, clips * length, width)
+    results = train_step(
+        own,
+        attend_weight[0],
+        merge_weight[0],
+        up_weight[0],
+        down_weight[0],
+        norm_gains[0],
+        offsets[0],
+        up_bias,
+        clips,
+        ways,
+        1,
+    )
+    section_outputs, gains, shifts, attend, merge, up, bias, down = results
+    return (
+        section_outputs.reshape(section_inputs.shape),
+        gains[None],
+        shifts[None],
+        attend[None],
+        merge[None],
+        up[None],
+        bias,
+        down[None],
+    )
+
+
 def solution(mesh):
     return jax.shard_map(
         body,

time: 1140 us -> 280 us (0.25); the launches traced: 1130 us -> 280 us
  waiting for transfers between devices: 564 us -> 0 us
  matrix products: 293 us -> 0 us
  Pallas kernels: 0 us -> 271 us
  local copies, waits for them, and re-layouts: 121 us -> 8.21 us
  blocking collectives: 75 us -> 0 us
  other arithmetic: 30 us -> 0 us
  starting transfers between devices: 25.8 us -> 0 us
  between operations: 20 us -> 0.66 us
    reduce_scatter x4 -> x0, waiting for transfers between devices: 391 us -> none  [the longest x1 116 us: body(): lax.psum_scatter(totals[2][None], 'fsdp', scatter_dimension=1, tiled=True)]
    dot_general x90 -> x0, matrix products: 293 us -> none  [the longest x5 56.5 us: layer_forward(): jnp.dot(normed_two, up_weight, preferred_element_type=jnp.float32)]
    pallas_call x0 -> x1, Pallas kernels: none -> 271 us  [train_step(): pl.pallas_call(functools.partial(relay_kernel, levels, clips, plan), out_...]
    all_gather x4 -> x0, waiting for transfers between devices: 76.3 us -> none  [the longest x1 42.3 us: body(): lax.all_gather(shards[3], 'fsdp', axis=1, tiled=True)]
    ppermute x8 -> x0, waiting for transfers between devices: 50.4 us -> none  [from_behind(): return lax.ppermute(block, axis, route)]
    unnamed x14 -> x0, waiting for transfers between devices: 46.4 us -> none
    all_gather x2 -> x0, blocking collectives: 39.1 us -> none  [the longest x1 19.9 us: body(): lax.all_gather(shards[4], 'fsdp', axis=2, tiled=True)]
    unnamed x1 -> x0, blocking collectives: 35.9 us -> none
  transfers between devices with their start and end apart: 19 -> 0, of which waited for: 15 -> 0; matrix products, arithmetic and copies ran while one was open for 16% -> 0% of each run, Pallas kernels for 0% -> 0%
where the time goes in v1:
time: 280 us
  Pallas kernels  271 us (97%)
  local copies, waits for them, and re-layouts  8.21 us (3%)
    pallas_call x1, Pallas kernels, train_step(): pl.pallas_call(functools.partial(relay_kernel, levels, clips, plan), out_...  271 us
    unnamed x20, local copies, waits for them, and re-layouts  8.21 us

profile of v1, /device:TPU:0, one launch (start us, length us, event | category | flops | bytes accessed | tf_op | source)
XLA Modules:
  0.0 280.1 jit_solution(9094018899497473694)
XLA Ops:
  0.6 271.3 %shard_map.143 = (bf16[4,256,768]{2,1,0:T(8,128)(2,1)}, f32[2,48]{1,0:T(2,128)}, f32[6,48]{1,0:T(8,128)}, f32[48,2304]{1,0:T(8,128)}, f32[48,768]{1,0:T(8,128)},...) custom-call(bf16[4,256,768]{2,1,0:T(8,128)(2,1)} %bitcast.14, bf16[48,2304]{1,0:T(8,128)(2,1)} %bitcast.21, ...), custom_call_target="tpu_custom_call" | custom-call | tf_op jit(solution)/shard_map/pallas_call | solution.py:867
  271.9 1.3 copy.16
  273.2 0.0 copy-start.5
  273.2 0.0 copy-start.2
  273.2 0.0 copy-start.3
  273.2 0.0 copy-start.1
  273.2 2.7 copy.24
  275.9 0.0 copy-done.5
  275.9 0.0 copy-start.4
  275.9 0.0 copy-start
  275.9 0.6 copy.25
  276.5 0.0 copy-done.2
  276.5 0.8 copy.26
  277.3 0.0 copy-done.3
  277.3 0.7 copy.27
  277.9 0.0 copy-done.1
  277.9 0.8 copy.28
  278.7 0.0 copy-done.4
  278.7 0.6 copy.29
  279.3 0.0 copy-done
  279.3 0.8 copy.30
Async XLA Ops:
  273.2 2.8 copy-start.5
  273.2 3.3 %copy-start.2 = (f32[48,2304]{1,0:T(8,128)S(1)}, f32[48,2304]{1,0:T(8,128)}, u32[]{:S(2)}) copy-start(f32[48,2304]{1,0:T(8,128)} %get-tuple-element.19) | copy-start | bytes 1327108
  273.2 4.1 %copy-start.3 = (f32[48,768]{1,0:T(8,128)S(1)}, f32[48,768]{1,0:T(8,128)}, u32[]{:S(2)}) copy-start(f32[48,768]{1,0:T(8,128)} %get-tuple-element.20) | copy-start | bytes 442372
  273.2 4.8 %copy-start.1 = (f32[48,3072]{1,0:T(8,128)S(1)}, f32[48,3072]{1,0:T(8,128)}, u32[]{:S(2)}) copy-start(f32[48,3072]{1,0:T(8,128)} %get-tuple-element.21) | copy-start | bytes 1769476
  275.9 2.8 %copy-start.4 = (f32[1,192]{1,0:T(1,128)S(1)}, f32[1,192]{1,0:T(1,128)}, u32[]{:S(2)}) copy-start(f32[1,192]{1,0:T(1,128)} %get-tuple-element.46) | copy-start | bytes 2308
  275.9 3.4 %copy-start = (f32[192,768]{1,0:T(8,128)S(1)}, f32[192,768]{1,0:T(8,128)}, u32[]{:S(2)}) copy-start(f32[192,768]{1,0:T(8,128)} %get-tuple-element.23) | copy-start | bytes 1769476

commit v2 on v1

--- a/solution.py
+++ b/solution.py
@@ -111,97 +111,125 @@
         pl.semaphore_wait(barrier, 5 - ends)
 
 
+class Piece:
+    def __init__(self, shard, ref, kind, start=0, size=None):
+        self.shard, self.ref, self.plain = shard, ref, kind == "level"
+        self.rows = None if size is None else pl.ds(start, size)
+
+    def block(self, index):
+        return self.ref.at[index] if self.rows is None else self.ref.at[index, self.rows]
+
+    def span(self, count):
+        return self.block(pl.ds(0, count))
+
+
 class Gather:
-    def __init__(self, place, shards, wholes, kinds, send_sem, recv_sem, local_sem):
-        self.place, self.shards, self.wholes, self.kinds = place, shards, wholes, kinds
+    def __init__(self, place, pieces, send_sem, recv_sem, local_sem):
+        self.place, self.pieces = place, pieces
         self.send_sem, self.recv_sem, self.local_sem = send_sem, recv_sem, local_sem
-        self.sends, self.local = Sends(), []
-
-    def send(self, piece, block, way, own=False, when=None):
-        target = self.wholes[piece](block)
-        copy = pltpu.make_async_remote_copy(
-            src_ref=self.shards[piece] if own else target,
+        self.side = 2 * place.levels
+
+    def copy(self, source, target, out_sem, in_sem, way):
+        return pltpu.make_async_remote_copy(
+            src_ref=source,
             dst_ref=target,
-            send_sem=self.send_sem.at[piece, block, way],
-            recv_sem=self.recv_sem.at[piece, block],
+            send_sem=out_sem,
+            recv_sem=in_sem,
             device_id=(self.place.section, self.place.targets[way]),
             device_id_type=MESH,
         )
-        self.sends.start(copy, when)
-
-    def arrived(self, piece, block, when=None):
-        target = self.wholes[piece](block)
-        copy = pltpu.make_async_remote_copy(
-            src_ref=target,
-            dst_ref=target,
-            send_sem=self.send_sem.at[piece, block, 0],
-            recv_sem=self.recv_sem.at[piece, block],
-            device_id=(self.place.section, self.place.targets[SIDE]),
-            device_id_type=MESH,
+
+    def send(self, piece, level, row, way, own=False, when=None):
+        held = self.pieces[piece]
+        target = held.block(self.place.block(level, row, self.place.core))
+        kind = {SIDE: 0, ACROSS: 1, UP: 2, DOWN: 2}[way]
+        copy = self.copy(
+            held.shard if own else target,
+            target,
+            self.send_sem.at[piece, kind],
+            self.recv_sem.at[piece, self.side if way == SIDE else level * 2 + row],
+            way,
         )
+        if when is None:
+            copy.start()
+        else:
+            pl.when(when)(copy.start)
+
+    def arrived(self, piece, level, row, when=None):
+        target = self.pieces[piece].block(self.place.block(level, row, self.place.core))
+        index = level * 2 + row
+        copy = self.copy(target, target, self.send_sem.at[piece, 0], self.recv_sem.at[piece, index], SIDE)
         if when is None:
             copy.wait_recv()
         else:
             pl.when(when)(copy.wait_recv)
 
-    def start(self):
-        mine = self.place.mine
-        for piece in range(len(self.shards)):
-            self.send(piece, mine, ACROSS, own=True)
-            self.send(piece, mine, UP, own=True, when=self.place.has_up)
-            self.send(piece, mine, DOWN, own=True, when=self.place.has_down)
-            self.send(piece, mine, SIDE, own=True)
-            copy = pltpu.make_async_copy(
-                self.shards[piece], self.wholes[piece](mine), self.local_sem.at[piece]
-            )
-            copy.start()
-            self.local.append(copy)
+    def local(self, piece):
+        held = self.pieces[piece]
+        return pltpu.make_async_copy(held.shard, held.block(self.place.mine), self.local_sem.at[piece])
+
+    def start(self, piece):
+        place = self.place
+        self.send(piece, place.level, place.row, ACROSS, own=True)
+        self.send(piece, place.level, place.row, UP, own=True, when=place.has_up)
+        self.send(piece, place.level, place.row, DOWN, own=True, when=place.has_down)
+        self.send(piece, place.level, place.row, SIDE, own=True)
+        self.local(piece).start()
 
     def first_across(self, piece):
-        block = self.place.mine ^ 2
-        self.arrived(piece, block)
-        self.send(piece, block, UP, when=self.place.has_up)
-        self.send(piece, block, DOWN, when=self.place.has_down)
-        self.send(piece, block, SIDE)
+        place = self.place
+        level, row = place.level, 1 - place.row
+        self.arrived(piece, level, row)
+        self.send(piece, level, row, UP, when=place.has_up)
+        self.send(piece, level, row, DOWN, when=place.has_down)
+        self.send(piece, level, row, SIDE)
 
     def from_levels(self, piece, distance):
         place = self.place
-        plain = self.kinds[piece] == "level"
+        plain = self.pieces[piece].plain
         for row in (place.row,) if plain else (place.row, 1 - place.row):
             for sign in (-1, 1):
                 other = place.level + sign * distance
                 here = other >= 0 if sign < 0 else other < place.levels
                 onward = place.has_up if sign < 0 else place.has_down
-                block = place.block(other, row, place.core)
-                self.arrived(piece, block, here)
+                self.arrived(piece, other, row, here)
                 if distance < place.levels - 1:
-                    self.send(piece, block, UP if sign < 0 else DOWN, when=jnp.logical_and(here, onward))
+                    way = UP if sign < 0 else DOWN
+                    self.send(piece, other, row, way, when=jnp.logical_and(here, onward))
                 if plain:
-                    self.send(piece, block, ACROSS, when=here)
-                self.send(piece, block, SIDE, when=here)
+                    self.send(piece, other, row, ACROSS, when=here)
+                self.send(piece, other, row, SIDE, when=here)
 
     def from_across(self, piece, distance):
         place = self.place
-        if self.kinds[piece] != "level":
+        if not self.pieces[piece].plain:
             return
         for sign in (-1, 1) if distance else (1,):
             other = place.level + sign * distance
             here = None
             if distance:
                 here = other >= 0 if sign < 0 else other < place.levels
-            block = place.block(other, 1 - place.row, place.core)
-            self.arrived(piece, block, here)
-            self.send(piece, block, SIDE, when=here)
+            self.arrived(piece, other, 1 - place.row, here)
+            self.send(piece, other, 1 - place.row, SIDE, when=here)
 
     def from_side(self, piece):
-        for level in range(self.place.levels):
-            for row in range(2):
-                self.arrived(piece, self.place.block(level, row, 1 - self.place.core))
-
-    def drain(self):
-        for copy in self.local:
-            copy.wait()
-        self.sends.drain()
+        span = self.pieces[piece].span(self.side)
+        self.copy(span, span, self.send_sem.at[piece, 0], self.recv_sem.at[piece, self.side], SIDE).wait_recv()
+
+    def drain(self, piece):
+        place, held = self.place, self.pieces[piece]
+
+        def sent(count, kind):
+            span = held.span(count)
+            return self.copy(span, span, self.send_sem.at[piece, kind], self.recv_sem.at[piece, 0], SIDE)
+
+        rows = 1 if held.plain else 2
+        self.local(piece).wait()
+        sent(self.side, 0).wait_send()
+        sent(place.levels if held.plain else 1, 1).wait_send()
+        inner = jnp.logical_and(place.has_up, place.has_down)
+        pl.when(inner)(sent(rows * (place.levels + 1), 2).wait_send)
+        pl.when(jnp.logical_not(inner))(sent(rows, 2).wait_send)
 
 
 class Chunk:
@@ -215,8 +243,7 @@
             self.side_in,
             self.across_out,
             self.across_in,
-            self.up_out,
-            self.down_out,
+            self.chain_out,
             self.chain_in,
         ) = sems
 
@@ -236,7 +263,7 @@
     def side(self, pair):
         block = pair * 2 + 1 - self.place.core
         return self.copy(
-            block, self.from_side.at[pair], self.side_out.at[pair], self.side_in.at[pair], SIDE
+            block, self.from_side.at[pair], self.side_out, self.side_in.at[pair], SIDE
         )
 
     def across(self, level, slot):
@@ -244,7 +271,7 @@
         return self.copy(
             block,
             self.from_across.at[slot],
-            self.across_out.at[slot],
+            self.across_out,
             self.across_in.at[slot],
             ACROSS,
         )
@@ -260,7 +287,7 @@
         return self.copy(
             self.place.block(target, row, self.place.core),
             self.from_chain.at[slot, index],
-            self.up_out.at[slot, target],
+            self.chain_out.at[slot],
             self.chain_in.at[slot, index],
             UP,
         )
@@ -270,7 +297,7 @@
         return self.copy(
             self.place.block(target, row, self.place.core),
             self.from_chain.at[slot, index],
-            self.down_out.at[slot, target],
+            self.chain_out.at[slot],
             self.chain_in.at[slot, index],
             DOWN,
         )
@@ -280,7 +307,7 @@
         pltpu.make_async_remote_copy(
             src_ref=target,
             dst_ref=target,
-            send_sem=self.side_out.at[0],
+            send_sem=self.side_out,
             recv_sem=self.chain_in.at[slot, index],
             device_id=(self.place.section, self.place.targets[SIDE]),
             device_id_type=MESH,
@@ -288,14 +315,18 @@
 
     def add(self, block, term):
         part = self.part(block)
-        total = part[...].astype(F32) + term.astype(F32)
-        part[...] = total.astype(part.dtype)
+        part[...] = part[...] + term
 
     def send_side(self):
         @pl.loop(0, self.levels * 2)
         def _(pair):
             self.side(pair).start()
 
+    def join_pair(self, level, row):
+        pair = level * 2 + row
+        self.side(pair).wait_recv()
+        self.add(pair * 2 + self.place.core, self.from_side[pair])
+
     def join_side(self):
         place = self.place
         for other in (True, False):
@@ -303,9 +334,7 @@
 
             @pl.loop(0, self.levels)
             def _(level):
-                pair = level * 2 + row
-                self.side(pair).wait_recv()
-                self.add(pair * 2 + place.core, self.from_side[pair])
+                self.join_pair(level, row)
                 if other and self.order == ACROSS_FIRST:
                     self.across(level, level).start()
 
@@ -378,22 +407,20 @@
             out(self.part(self.place.mine)[...].astype(F32) + self.from_across[0].astype(F32))
 
     def drain(self):
-        @pl.loop(0, self.levels * 2)
-        def _(pair):
-            self.side(pair).wait_send()
-
-        if self.order == ACROSS_FIRST:
-
-            @pl.loop(0, self.levels)
-            def _(level):
-                self.across(level, level).wait_send()
-
-        else:
-            self.across(self.place.level, 0).wait_send()
-        for slot, row in self.rows():
-            for target in range(self.levels):
-                pl.when(self.place.level < target)(self.up(row, slot, target).wait_send)
-                pl.when(self.place.level > target)(self.down(row, slot, target).wait_send)
+        def sent(span, out_sem):
+            pltpu.make_async_remote_copy(
+                src_ref=span,
+                dst_ref=span,
+                send_sem=out_sem,
+                recv_sem=self.side_in.at[0],
+                device_id=(self.place.section, self.place.targets[SIDE]),
+                device_id_type=MESH,
+            ).wait_send()
+
+        sent(self.from_side, self.side_out)
+        sent(self.from_across, self.across_out)
+        for slot, _ in self.rows():
+            sent(self.from_chain.at[slot, pl.ds(0, self.levels - 1)], self.chain_out.at[slot])
 
 
 def chunk_scratch(levels, order, rows, cols, dtype, shared):
@@ -405,17 +432,16 @@
     return from_side + [
         pltpu.VMEM((crossing,) + block, dtype),
         pltpu.VMEM((slots, levels + 1) + block, dtype),
+        dma(()),
         dma((levels * 2,)),
-        dma((levels * 2,)),
+        dma(()),
         dma((crossing,)),
-        dma((crossing,)),
-        dma((slots, levels)),
-        dma((slots, levels)),
+        dma((slots,)),
         dma((slots, levels + 1)),
     ]
 
 
-CHUNK_REFS = 9
+CHUNK_REFS = 8
 
 
 def pad_lanes(rows, lanes=128):
@@ -479,8 +505,9 @@
         recv_sem,
         out_sem,
         free_sem,
-    ) = refs[16:47]
-    chunk_refs = list(refs[47:])
+        store_sem,
+    ) = refs[16:48]
+    chunk_refs = list(refs[48:])
     place = Place(levels)
     section, mine = place.section, place.mine
     batches, rows, width = own.shape
@@ -500,26 +527,18 @@
     place.greet()
 
     half_share = wide_share // 2
-    shards = [
-        packed,
-        attend_shard,
-        up_shard,
-        merge_shard,
-        down_shard.at[pl.ds(0, half_share)],
-        down_shard.at[pl.ds(half_share, half_share)],
+    pieces = [
+        Piece(packed, vector_blocks, "level"),
+        Piece(attend_shard, attend_blocks, "level"),
+        Piece(up_shard, up_blocks, "level"),
+        Piece(merge_shard, merge_blocks, "level"),
+        Piece(down_shard.at[pl.ds(0, half_share)], down_blocks, "level", 0, half_share),
+        Piece(down_shard.at[pl.ds(half_share, half_share)], down_blocks, "across", half_share, half_share),
     ]
-    wholes = [
-        lambda block: vector_blocks.at[block],
-        lambda block: attend_blocks.at[block],
-        lambda block: up_blocks.at[block],
-        lambda block: merge_blocks.at[block],
-        lambda block: down_blocks.at[block, pl.ds(0, half_share)],
-        lambda block: down_blocks.at[block, pl.ds(half_share, half_share)],
-    ]
-    kinds = ["level"] * 5 + ["across"]
-    gather = Gather(place, shards, wholes, kinds, gather_send, gather_recv, gather_local)
-    count = len(shards)
-    gather.start()
+    gather = Gather(place, pieces, gather_send, gather_recv, gather_local)
+    count = len(pieces)
+    for piece in range(count):
+        gather.start(piece)
     gather.first_across(count - 1)
     for distance in range(1, levels):
         for piece in range(count):
@@ -529,7 +548,8 @@
         gather.from_across(piece, levels - 1)
     for piece in range(count):
         gather.from_side(piece)
-    gather.drain()
+    for piece in range(count):
+        gather.drain(piece)
     vectors[...] = jnp.concatenate([vector_blocks[block, 0:8, 0:share] for block in range(ways)], axis=1)
     bias[...] = jnp.concatenate(
         [unfold(vector_blocks[block, 8:16], wide_share) for block in range(ways)], axis=1
@@ -538,9 +558,9 @@
     def flat(blocks):
         return blocks.reshape(-1, blocks.shape[-1])
 
-    def relay(batch):
+    def relay(batch, slot=0):
         return pltpu.make_async_remote_copy(
-            src_ref=leaving.at[batch],
+            src_ref=leaving.at[slot],
             dst_ref=entry.at[1, batch],
             send_sem=send_sem.at[batch],
             recv_sem=recv_sem.at[batch],
@@ -548,8 +568,8 @@
             device_id_type=MESH,
         )
 
-    def keep(batch):
-        return pltpu.make_async_copy(leaving.at[batch], out.at[batch], out_sem.at[batch])
+    def keep(batch, slot=0):
+        return pltpu.make_async_copy(leaving.at[slot], out.at[batch], out_sem.at[batch])
 
     vector_sum[...] = jnp.zeros_like(vector_sum)
     bias_sum[...] = jnp.zeros_like(bias_sum)
@@ -562,7 +582,7 @@
         at = pl.multiple_of(batch * 4 * length + (index % 2) * 2 * length, 128)
         return probability.at[pl.ds((index // 2) * length, length), pl.ds(at, 2 * length)]
 
-    def forward(batch):
+    def forward(batch, slot):
         normal, _ = standard(entry[fed, batch].astype(F32))
         normed[batch] = (normal * row(0) + row(2)).astype(BF)
         for part, shift in ((0, 4), (1, None), (2, 5)):
@@ -600,9 +620,9 @@
             activated[batch, :, at] = value.astype(BF)
             slope[batch, :, at] = rate.astype(BF)
         result = temp[...] + matmul(activated[batch], flat(down_blocks[...])) + row(7)
-        leaving[batch] = result.astype(BF)
-
-    def backward(batch):
+        leaving[slot] = result.astype(BF)
+
+    def backward(batch, slot, between):
         low = entry[back, batch]
         vector_sum[7:8] += column_sum(low.astype(F32))
         blocks = 4
@@ -612,6 +632,7 @@
             rate = rate * slope[batch, :, at].astype(F32)
             bias_sum[:, at] += column_sum(rate)
             slope[batch, :, at] = rate.astype(BF)
+        between()
         temp[...] = matmul(slope[batch], flat(up_blocks[...]), NT)
         normal, scale = standard(middle[batch].astype(F32))
         grad = temp[...]
@@ -650,29 +671,9 @@
         grad = temp[...]
         vector_sum[0:1] += column_sum(grad * normal)
         vector_sum[2:3] += column_sum(grad)
-        leaving[batch] = (sum_temp[...] + norm_back(grad * row(0), normal, scale)).astype(BF)
+        leaving[slot] = (sum_temp[...] + norm_back(grad * row(0), normal, scale)).astype(BF)
 
     load_own.wait()
-
-    @pl.loop(0, 2 * batches)
-    def _(step):
-        is_forward = jnp.where(section == 0, step < batches, lax.rem(step, 2) == 0)
-        batch = jnp.where(section == 0, lax.rem(step, batches), lax.div(step, 2))
-
-        @pl.when(is_forward)
-        def _():
-            pl.when(section == 1)(relay(batch).wait_recv)
-            forward(batch)
-            pl.when(section == 0)(relay(batch).start)
-            pl.when(section == 1)(keep(batch).start)
-
-        @pl.when(jnp.logical_not(is_forward))
-        def _():
-            pl.when(section == 0)(relay(batch).wait)
-            pl.when(section == 1)(keep(batch).wait)
-            backward(batch)
-            pl.when(section == 1)(relay(batch).start)
-            pl.when(section == 0)(keep(batch).start)
 
     chunks = []
     part_refs = [vector_blocks, attend_blocks, merge_blocks, up_blocks, down_blocks]
@@ -685,9 +686,86 @@
         chunks.append(Chunk(place, order, part_refs[which], start, [from_side] + held[:2], held[2:]))
     down_a, down_b, up_a, up_b, attend_a, attend_b, merge, vector = chunks
 
-    def store(target, chunk):
+    def down_gradient():
+        def pair_at(index):
+            late = lax.div(index, levels)
+            return lax.rem(index, levels), jnp.where(late == 0, 1 - place.row, place.row), late == 0
+
+        def multiply(index):
+            level, row, _ = pair_at(index)
+            pair = level * 2 + row
+            at = pl.ds(pl.multiple_of(pair * 2 * wide_share, 128), 2 * wide_share)
+            tile = flat(activated[:, :, at])
+            for chunk in (down_a, down_b):
+                at = pl.ds(chunk.start, chunk.cols)
+                product = matmul(tile, flat(entry[back, :, :, at]), TN).astype(BF)
+                for core in range(2):
+                    down_blocks[pair * 2 + core, :, at] = product[core * wide_share : (core + 1) * wide_share]
+                chunk.side(pair).start()
+
+        def join(index):
+            level, row, early = pair_at(index)
+            down_a.join_pair(level, row)
+            down_b.join_pair(level, row)
+            pl.when(early)(down_b.across(level, level).start)
+
+        multiply(jnp.int32(0))
+
+        @pl.loop(1, 2 * levels)
+        def _(index):
+            multiply(index)
+            join(index - 1)
+
+        join(jnp.int32(2 * levels - 1))
+        down_a.chain_start()
+
+    @pl.loop(0, 2 * batches)
+    def _(step):
+        is_forward = jnp.where(section == 0, step < batches, lax.rem(step, 2) == 0)
+        batch = jnp.where(section == 0, lax.rem(step, batches), lax.div(step, 2))
+
+        slot = jnp.where(section == 0, lax.rem(batch, 2), jnp.where(is_forward, 0, 1))
+
+        @pl.when(is_forward)
+        def _():
+            pl.when(section == 1)(relay(batch).wait_recv)
+            pl.when(jnp.logical_and(section == 0, batch >= 2))(relay(batch - 2).wait_send)
+            pl.when(jnp.logical_and(section == 1, batch >= 1))(keep(batch - 1).wait)
+            forward(batch, slot)
+            pl.when(section == 0)(relay(batch, slot).start)
+            pl.when(section == 1)(keep(batch, slot).start)
+
+        @pl.when(jnp.logical_not(is_forward))
+        def _():
+            pl.when(section == 0)(relay(batch).wait_recv)
+            pl.when(jnp.logical_and(section == 0, batch < 2))(relay(batch + batches - 2).wait_send)
+            pl.when(jnp.logical_and(section == 0, batch >= 2))(keep(batch - 2).wait)
+            pl.when(jnp.logical_and(section == 1, batch >= 1))(relay(batch - 1).wait_send)
+            last = jnp.logical_and(section == 0, step == 2 * batches - 1)
+            backward(batch, slot, lambda: pl.when(last)(down_gradient))
+            pl.when(section == 1)(relay(batch, slot).start)
+            pl.when(section == 0)(keep(batch, slot).start)
+
+    pl.when(section == 1)(down_gradient)
+    stores = []
+
+    def store(target, chunk, through=None, first=0):
         def put(value):
-            target[:, pl.ds(chunk.start, chunk.cols)] = value
+            if through is None:
+                target[:, pl.ds(chunk.start, chunk.cols)] = value
+                return
+            done = 0
+            while done < chunk.cols:
+                column = chunk.start + done
+                size = min(width - column % width, chunk.cols - done)
+                at = (pl.ds(first + column // width * share, share), pl.ds(column % width, size))
+                through[at] = value[:, done : done + size]
+                copy = pltpu.make_async_copy(
+                    through.at[at], target.at[:, pl.ds(column, size)], store_sem.at[len(stores)]
+                )
+                copy.start()
+                stores.append(copy)
+                done += size
 
         return put
 
@@ -714,29 +792,14 @@
             free_sem.at[index], inc=1, device_id=(section, place.targets[SIDE]), device_id_type=MESH
         )
 
-    pair_cols = 2 * wide_share
-
-    @pl.loop(0, levels * 2)
-    def _(pair):
-        tile = flat(activated[:, :, pl.ds(pl.multiple_of(pair * pair_cols, 128), pair_cols)])
-        for chunk in (down_a, down_b):
-            at = pl.ds(chunk.start, chunk.cols)
-            product = matmul(tile, flat(entry[back, :, :, at]), TN).astype(BF)
-            for core in range(2):
-                down_blocks[pair * 2 + core, :, at] = product[core * wide_share : (core + 1) * wide_share]
-            chunk.side(pair).start()
-
     for block in range(ways):
         vector_blocks[block, 0:8] = pad_lanes(vector_sum[:, block * share : (block + 1) * share])
         vector_blocks[block, 8:16] = fold(bias_sum[:, block * wide_share : (block + 1) * wide_share])
     vector.send_side()
-    down_a.join_side()
-    down_a.chain_start()
-    down_b.join_side()
-    vector.join_side()
     turned = turn(normed_two, 0)
     columns(turned, slope, up_a)
     columns(turned, slope, up_b)
+    vector.join_side()
     up_a.join_side()
     release(0)
     down_a.chain_pass(1)
@@ -751,8 +814,9 @@
     vector.chain_start()
     columns(turned, projected, attend_b, 1)
     attend_a.join_side()
+    release(2)
     turned = turn(attended, 0)
-    columns(turned, middle, merge)
+    columns(turned, middle, merge, 2)
     attend_b.join_side()
     down_b.chain_pass(1)
     merge.join_side()
@@ -773,34 +837,58 @@
 
     def store_vectors(value):
         gain_out[...] = value[0:2, :share]
-        shift_out[...] = value[2:8, :share]
+        for index in range(6):
+            shift_out[index] = value[2 + index : 3 + index, :share]
         bias_out[...] = unfold(value[8:16], wide_share)
 
     vector.chain_end(store_vectors)
-    up_a.chain_end(store(up_out, up_a))
+    up_a.chain_end(store(up_out, up_a, temp, 0))
     up_b.chain_pass(2)
     attend_a.chain_pass(1)
     attend_b.join_across()
     attend_b.chain_start()
-    up_b.chain_end(store(up_out, up_b))
+    up_b.chain_end(store(up_out, up_b, temp, 0))
     attend_a.chain_pass(2)
     attend_b.chain_pass(1)
     merge.join_across()
     merge.chain_start()
-    attend_a.chain_end(store(attend_out, attend_a))
+    attend_a.chain_end(store(attend_out, attend_a, sum_temp, 0))
     attend_b.chain_pass(2)
     merge.chain_pass(1)
-    attend_b.chain_end(store(attend_out, attend_b))
+    attend_b.chain_end(store(attend_out, attend_b, sum_temp, 0))
     merge.chain_pass(2)
     down_a.finish(store(down_out, down_a))
-    merge.chain_end(store(merge_out, merge))
+    merge.chain_end(store(merge_out, merge, sum_temp, 3 * share))
     for chunk in chunks:
         chunk.drain()
 
-    @pl.loop(0, batches)
-    def _(batch):
-        pl.when(section == 1)(relay(batch).wait_send)
-        pl.when(section == 0)(keep(batch).wait)
+    for copy in stores:
+        copy.wait()
+
+    @pl.when(section == 0)
+    def _():
+        keep(batches - 2).wait()
+        keep(batches - 1).wait()
+
+    @pl.when(section == 1)
+    def _():
+        keep(batches - 1).wait()
+        relay(batches - 1).wait_send()
+
+
+def settle_kernel(*refs):
+    count = (len(refs) - 2) // 3
+    load_sem, store_sem = refs[-2:]
+    sources, targets, held = refs[:count], refs[count : 2 * count], refs[2 * count : 3 * count]
+    loads = [pltpu.make_async_copy(sources[i], held[i], load_sem.at[i]) for i in range(count)]
+    stores = [pltpu.make_async_copy(held[i], targets[i], store_sem.at[i]) for i in range(count)]
+    for copy in loads:
+        copy.start()
+    for load, store in zip(loads, stores):
+        load.wait()
+        store.start()
+    for copy in stores:
+        copy.wait()
 
 
 def train_step(own, attend, merge, up, down, gains, shifts, bias, clips, ways, collective_id):
@@ -816,7 +904,7 @@
         (3, wide // 2, ACROSS_FIRST, share, wide // 2, BF, None),
         (1, 0, ACROSS_FIRST, share, 3 * width // 2, BF, 2),
         (1, 3 * width // 2, ACROSS_FIRST, share, 3 * width // 2, BF, 3),
-        (2, 0, ACROSS_FIRST, share, width, BF, None),
+        (2, 0, ACROSS_FIRST, share, width, BF, 2),
         (0, 0, ACROSS_FIRST, 16, 128, F32, None),
     ]
     dma = pltpu.SemaphoreType.DMA
@@ -845,18 +933,19 @@
         held(width),
         held(wide),
         held(wide),
-        held(width),
+        pltpu.VMEM((2, rows, width), BF),
         pltpu.VMEM((rows, width), BF),
         pltpu.VMEM((rows, width), F32),
         pltpu.VMEM((rows, width), F32),
-        dma((6, ways, 4)),
-        dma((6, ways)),
+        dma((6, 3)),
+        dma((6, 2 * levels + 1)),
         dma((6,)),
         dma(()),
         dma((batches,)),
         dma((batches,)),
         dma((batches,)),
-        pltpu.SemaphoreType.REGULAR((2,)),
+        pltpu.SemaphoreType.REGULAR((3,)),
+        dma((9,)),
     ]
     for _, _, order, chunk_rows, cols, dtype, shared in plan:
         scratch += chunk_scratch(levels, order, chunk_rows, cols, dtype, shared is not None)
@@ -864,12 +953,12 @@
     def grad(*shape):
         return jax.ShapeDtypeStruct(shape, F32)
 
-    return pl.pallas_call(
+    results = pl.pallas_call(
         functools.partial(relay_kernel, levels, clips, plan),
         out_shape=[
             jax.ShapeDtypeStruct(own.shape, BF),
             grad(2, share),
-            grad(6, share),
+            grad(6, 1, share),
             grad(share, 3 * width),
             grad(share, width),
             grad(share, wide),
@@ -877,12 +966,20 @@
             grad(wide_share, width),
         ],
         in_specs=[anywhere] * 5 + [vmem] * 3,
-        out_specs=[anywhere] + [vmem] * 7,
+        out_specs=[anywhere, vmem, vmem, anywhere, anywhere, anywhere, vmem, vmem],
         scratch_shapes=scratch,
         compiler_params=pltpu.CompilerParams(
-            collective_id=collective_id, has_side_effects=True, vmem_limit_bytes=63 * 2**20
+            collective_id=collective_id, has_side_effects=True, vmem_limit_bytes=62 * 2**20
         ),
     )(own, attend, merge, up, down, gains, shifts, bias)
+    return pl.pallas_call(
+        settle_kernel,
+        out_shape=[jax.ShapeDtypeStruct(result.shape, result.dtype) for result in results],
+        in_specs=[anywhere] * len(results),
+        out_specs=[anywhere] * len(results),
+        scratch_shapes=[pltpu.VMEM(result.shape, result.dtype) for result in results]
+        + [dma((len(results),))] * 2,
+    )(*results)
 
 
 def from_behind(block, axis, distance):
@@ -1198,7 +1295,7 @@
     return (
         section_outputs.reshape(section_inputs.shape),
         gains[None],
-        shifts[None],
+        shifts.swapaxes(0, 1),
         attend[None],
         merge[None],
         up[None],

time: 280 us -> 266 us (0.950)
  local copies, waits for them, and re-layouts: 8.21 us -> 0 us
  Pallas kernels: 271 us -> 265 us
    pallas_call x1, Pallas kernels: 271 us -> 262 us  [train_step(): pl.pallas_call(functools.partial(relay_kernel, levels, clips, plan), out_...]
    unnamed x20 -> x0, local copies, waits for them, and re-layouts: 8.21 us -> none
    pallas_call x0 -> x1, Pallas kernels: none -> 3.28 us  [train_step(): pl.pallas_call(settle_kernel, out_shape=[jax.ShapeDtypeStruct(result.shap...]
where the time goes in v2:
time: 266 us
  Pallas kernels  265 us (100%)
    pallas_call x1, Pallas kernels, train_step(): pl.pallas_call(functools.partial(relay_kernel, levels, clips, plan), out_...  262 us

profile of v2, /device:TPU:0, one launch (start us, length us, event | category | flops | bytes accessed | tf_op | source)
XLA Modules:
  0.0 265.8 jit_solution(7364061185192614535)
XLA Ops:
  0.6 261.8 %shard_map.143 = (bf16[4,256,768]{2,1,0:T(8,128)(2,1)}, f32[2,48]{1,0:T(2,128)}, f32[6,1,48]{2,1,0:T(1,128)}, f32[48,2304]{1,0:T(8,128)}, f32[48,768]{1,0:T(8,12...) custom-call(bf16[4,256,768]{2,1,0:T(8,128)(2,1)} %bitcast.14, bf16[48,2304]{1,0:T(8,128)(2,1)} %bitcast.17, ...), custom_call_target="tpu_custom_call" | custom-call | tf_op jit(solution)/shard_map/pallas_call | solution.py:956
  262.4 3.3 %shard_map.144 = (bf16[4,256,768]{2,1,0:T(8,128)(2,1)}, f32[2,48]{1,0:T(2,128)}, f32[6,1,48]{2,1,0:T(1,128)}, f32[48,2304]{1,0:T(8,128)}, f32[48,768]{1,0:T(8,12...) custom-call(bf16[4,256,768]{2,1,0:T(8,128)(2,1)} %get-tuple-element.24.refs_0_, ...), custom_call_target="tpu_custom_call" | custom-call | tf_op jit(solution)/shard_map/pallas_call | solution.py:975

commit v3 on v2

--- a/solution.py
+++ b/solution.py
@@ -213,6 +213,7 @@
             self.send(piece, other, 1 - place.row, SIDE, when=here)
 
     def from_side(self, piece):
+        self.local(piece).wait()
         span = self.pieces[piece].span(self.side)
         self.copy(span, span, self.send_sem.at[piece, 0], self.recv_sem.at[piece, self.side], SIDE).wait_recv()
 
@@ -224,7 +225,6 @@
             return self.copy(span, span, self.send_sem.at[piece, kind], self.recv_sem.at[piece, 0], SIDE)
 
         rows = 1 if held.plain else 2
-        self.local(piece).wait()
         sent(self.side, 0).wait_send()
         sent(place.levels if held.plain else 1, 1).wait_send()
         inner = jnp.logical_and(place.has_up, place.has_down)
@@ -327,36 +327,41 @@
         self.side(pair).wait_recv()
         self.add(pair * 2 + self.place.core, self.from_side[pair])
 
+    def level_at(self, index):
+        return jnp.where(self.place.level < self.levels // 2, self.levels - 1 - index, index)
+
     def join_side(self):
         place = self.place
         for other in (True, False):
             row = 1 - place.row if other else place.row
 
             @pl.loop(0, self.levels)
-            def _(level):
+            def _(index):
+                level = self.level_at(index)
                 self.join_pair(level, row)
                 if other and self.order == ACROSS_FIRST:
                     self.across(level, level).start()
 
+    def chain_open(self, row, slot, target):
+        level, last = self.place.level, self.levels - 1
+        pl.when(jnp.logical_and(level == 0, target > 0))(lambda: self.up(row, slot, target).start())
+        pl.when(jnp.logical_and(level == last, target < last))(
+            lambda: self.down(row, slot, target).start()
+        )
+
     def join_across(self):
         place = self.place
 
         @pl.loop(0, self.levels)
-        def _(level):
+        def _(index):
+            level = self.level_at(index)
             self.across(level, level).wait_recv()
             self.add(place.block(level, place.row, place.core), self.from_across[level])
+            self.chain_open(place.row, 0, level)
 
     def rows(self):
         row = self.place.row
         return ((0, row), (1, 1 - row)) if self.order == LEVELS_FIRST else ((0, row),)
-
-    def chain_start(self):
-        level, last = self.place.level, self.levels - 1
-        for slot, row in self.rows():
-            for target in range(self.levels):
-                if target:
-                    pl.when(level == 0)(self.up(row, slot, self.levels - target).start)
-                    pl.when(level == last)(self.down(row, slot, target - 1).start)
 
     def chain_pass(self, distance):
         place, last = self.place, self.levels - 1
@@ -442,6 +447,7 @@
 
 
 CHUNK_REFS = 8
+STEP = 512
 
 
 def pad_lanes(rows, lanes=128):
@@ -530,44 +536,47 @@
     pieces = [
         Piece(packed, vector_blocks, "level"),
         Piece(attend_shard, attend_blocks, "level"),
+        Piece(merge_shard, merge_blocks, "level"),
         Piece(up_shard, up_blocks, "level"),
-        Piece(merge_shard, merge_blocks, "level"),
         Piece(down_shard.at[pl.ds(0, half_share)], down_blocks, "level", 0, half_share),
         Piece(down_shard.at[pl.ds(half_share, half_share)], down_blocks, "across", half_share, half_share),
     ]
     gather = Gather(place, pieces, gather_send, gather_recv, gather_local)
-    count = len(pieces)
-    for piece in range(count):
-        gather.start(piece)
-    gather.first_across(count - 1)
-    for distance in range(1, levels):
-        for piece in range(count):
-            gather.from_levels(piece, distance)
-            gather.from_across(piece, distance - 1)
-    for piece in range(count):
-        gather.from_across(piece, levels - 1)
-    for piece in range(count):
-        gather.from_side(piece)
-    for piece in range(count):
-        gather.drain(piece)
-    vectors[...] = jnp.concatenate([vector_blocks[block, 0:8, 0:share] for block in range(ways)], axis=1)
-    bias[...] = jnp.concatenate(
-        [unfold(vector_blocks[block, 8:16], wide_share) for block in range(ways)], axis=1
-    )
-
     def flat(blocks):
         return blocks.reshape(-1, blocks.shape[-1])
 
-    def relay(batch, slot=0):
+    half = rows // 2 if clips % 2 == 0 else rows
+    portions = rows // half
+
+    def relay_part(batch, portion, slot=0):
+        here = pl.ds(portion * half, half)
         return pltpu.make_async_remote_copy(
-            src_ref=leaving.at[slot],
-            dst_ref=entry.at[1, batch],
-            send_sem=send_sem.at[batch],
-            recv_sem=recv_sem.at[batch],
+            src_ref=leaving.at[slot, here],
+            dst_ref=entry.at[1, batch, here],
+            send_sem=send_sem.at[batch, portion],
+            recv_sem=recv_sem.at[batch, portion],
             device_id=(1 - section, mine),
             device_id_type=MESH,
         )
 
+    class Relay:
+        def __init__(self, batch, slot=0):
+            self.copies = [relay_part(batch, portion, slot) for portion in range(portions)]
+
+        def start(self):
+            for copy in self.copies:
+                copy.start()
+
+        def wait_send(self):
+            for copy in self.copies:
+                copy.wait_send()
+
+        def wait_recv(self):
+            for copy in self.copies:
+                copy.wait_recv()
+
+    relay = Relay
+
     def keep(batch, slot=0):
         return pltpu.make_async_copy(leaving.at[slot], out.at[batch], out_sem.at[batch])
 
@@ -578,21 +587,23 @@
     def row(index):
         return vectors[index : index + 1, :]
 
-    def chances(batch, index):
-        at = pl.multiple_of(batch * 4 * length + (index % 2) * 2 * length, 128)
-        return probability.at[pl.ds((index // 2) * length, length), pl.ds(at, 2 * length)]
-
-    def forward(batch, slot):
-        normal, _ = standard(entry[fed, batch].astype(F32))
-        normed[batch] = (normal * row(0) + row(2)).astype(BF)
+    def chances(batch, start, pair):
+        at = pl.multiple_of(batch * 4 * length + (pair % 2) * 2 * length, 128)
+        first = start * (pairs // 2) + (pair // 2) * length
+        return probability.at[pl.ds(first, length), pl.ds(at, 2 * length)]
+
+    def attend_part(batch, start, size):
+        here = pl.ds(start, size)
+        normal, _ = standard(entry[fed, batch, here].astype(F32))
+        normed[batch, here] = (normal * row(0) + row(2)).astype(BF)
         for part, shift in ((0, 4), (1, None), (2, 5)):
             at = slice(part * width, (part + 1) * width)
-            value = matmul(normed[batch], flat(attend_blocks[:, :, at]))
+            value = matmul(normed[batch, here], flat(attend_blocks[:, :, at]))
             if shift is not None:
                 value = value + row(shift)
-            projected[batch, :, at] = value.astype(BF)
-        for clip in range(clips):
-            span = slice(clip * length, (clip + 1) * length)
+            projected[batch, here, at] = value.astype(BF)
+        for clip in range(size // length):
+            span = pl.ds(start + clip * length, length)
             for pair in range(pairs):
                 lanes = [slice(p * width + pair * 128, p * width + pair * 128 + 128) for p in range(3)]
                 query = projected[batch, span, lanes[0]] * jnp.asarray(HEAD_DIM**-0.5, BF)
@@ -603,55 +614,66 @@
                     exponent = jnp.exp(half - jnp.max(half, axis=-1, keepdims=True))
                     parts.append(exponent * (1.0 / jnp.sum(exponent, axis=-1, keepdims=True)))
                 weight = jnp.concatenate(parts, axis=1).astype(BF)
-                chances(batch, clip * pairs + pair)[...] = weight
+                chances(batch, start + clip * length, pair)[...] = weight
                 value = pair_parts(projected[batch, span, lanes[2]])
                 attended[batch, span, lanes[0]] = matmul(weight, value).astype(BF)
-        joined = matmul(attended[batch], flat(merge_blocks[...])) + row(6)
-        temp[...] = entry[fed, batch].astype(F32) + joined
-        middle[batch] = temp[...].astype(BF)
-        normal, _ = standard(temp[...])
-        normed_two[batch] = (normal * row(1) + row(3)).astype(BF)
+        joined = matmul(attended[batch, here], flat(merge_blocks[...])) + row(6)
+        temp[here] = entry[fed, batch, here].astype(F32) + joined
+        middle[batch, here] = temp[here].astype(BF)
+        normal, _ = standard(temp[here])
+        normed_two[batch, here] = (normal * row(1) + row(3)).astype(BF)
+
+    def rise_part(batch, start, size):
+        here = pl.ds(start, size)
         tile = 256
-        for start in range(0, wide, tile):
-            at = slice(start, start + tile)
+        for first in range(0, wide, tile):
+            at = slice(first, first + tile)
             value, rate = gelu_and_slope(
-                matmul(normed_two[batch], flat(up_blocks[:, :, at])) + bias[:, at]
+                matmul(normed_two[batch, here], flat(up_blocks[:, :, at])) + bias[:, at]
             )
-            activated[batch, :, at] = value.astype(BF)
-            slope[batch, :, at] = rate.astype(BF)
-        result = temp[...] + matmul(activated[batch], flat(down_blocks[...])) + row(7)
-        leaving[slot] = result.astype(BF)
-
-    def backward(batch, slot, between):
-        low = entry[back, batch]
+            activated[batch, here, at] = value.astype(BF)
+            slope[batch, here, at] = rate.astype(BF)
+
+    def fall_part(batch, start, size, slot):
+        here = pl.ds(start, size)
+        result = temp[here] + matmul(activated[batch, here], flat(down_blocks[...])) + row(7)
+        leaving[slot, here] = result.astype(BF)
+
+    def forward(batch, start, size, slot):
+        attend_part(batch, start, size)
+        rise_part(batch, start, size)
+        fall_part(batch, start, size, slot)
+
+    def backward(batch, start, size, slot):
+        here = pl.ds(start, size)
+        low = entry[back, batch, here]
         vector_sum[7:8] += column_sum(low.astype(F32))
         blocks = 4
         for block in range(0, ways, blocks):
             at = slice(block * wide_share, (block + blocks) * wide_share)
             rate = matmul(low, flat(down_blocks[block : block + blocks]), NT)
-            rate = rate * slope[batch, :, at].astype(F32)
+            rate = rate * slope[batch, here, at].astype(F32)
             bias_sum[:, at] += column_sum(rate)
-            slope[batch, :, at] = rate.astype(BF)
-        between()
-        temp[...] = matmul(slope[batch], flat(up_blocks[...]), NT)
-        normal, scale = standard(middle[batch].astype(F32))
-        grad = temp[...]
+            slope[batch, here, at] = rate.astype(BF)
+        temp[here] = matmul(slope[batch, here], flat(up_blocks[...]), NT)
+        normal, scale = standard(middle[batch, here].astype(F32))
+        grad = temp[here]
         vector_sum[1:2] += column_sum(grad * normal)
         vector_sum[3:4] += column_sum(grad)
-        grad = entry[back, batch].astype(F32) + norm_back(grad * row(1), normal, scale)
-        sum_temp[...] = grad
+        grad = entry[back, batch, here].astype(F32) + norm_back(grad * row(1), normal, scale)
+        sum_temp[here] = grad
         vector_sum[6:7] += column_sum(grad)
-        middle[batch] = grad.astype(BF)
-        low_temp[...] = matmul(middle[batch], flat(merge_blocks[...]), NT).astype(BF)
-        for clip in range(clips):
-            span = slice(clip * length, (clip + 1) * length)
+        middle[batch, here] = grad.astype(BF)
+        low_temp[here] = matmul(middle[batch, here], flat(merge_blocks[...]), NT).astype(BF)
+        for clip in range(size // length):
+            span = pl.ds(start + clip * length, length)
             for pair in range(pairs):
                 lanes = [slice(p * width + pair * 128, p * width + pair * 128 + 128) for p in range(3)]
                 query = projected[batch, span, lanes[0]]
                 key = pair_parts(projected[batch, span, lanes[1]])
                 value = pair_parts(projected[batch, span, lanes[2]])
                 upper = low_temp[span, lanes[0]]
-                weight = chances(batch, clip * pairs + pair)[...]
+                weight = chances(batch, start + clip * length, pair)[...]
                 rise = matmul(upper, value, NT)
                 value_grad = pair_join(matmul(weight, upper, TN))
                 parts = []
@@ -666,14 +688,44 @@
                 vector_sum[5:6, lanes[0]] += column_sum(value_grad)
                 for at, piece in zip(lanes, (query_grad, key_grad, value_grad)):
                     projected[batch, span, at] = piece.astype(BF)
-        temp[...] = matmul(projected[batch], flat(attend_blocks[...]), NT)
-        normal, scale = standard(entry[fed, batch].astype(F32))
-        grad = temp[...]
+        temp[here] = matmul(projected[batch, here], flat(attend_blocks[...]), NT)
+        normal, scale = standard(entry[fed, batch, here].astype(F32))
+        grad = temp[here]
         vector_sum[0:1] += column_sum(grad * normal)
         vector_sum[2:3] += column_sum(grad)
-        leaving[slot] = (sum_temp[...] + norm_back(grad * row(0), normal, scale)).astype(BF)
-
+        leaving[slot, here] = (sum_temp[here] + norm_back(grad * row(0), normal, scale)).astype(BF)
+
+    count = len(pieces)
+    early, late = range(3), range(4, count)
+    for piece in range(count):
+        gather.start(piece)
+    gather.first_across(count - 1)
+    for distance in range(1, levels - 1):
+        for piece in range(count):
+            gather.from_levels(piece, distance)
+            gather.from_across(piece, distance - 1)
+    for piece in range(4):
+        gather.from_levels(piece, levels - 1)
+        gather.from_across(piece, levels - 2)
+    for piece in early:
+        gather.from_across(piece, levels - 1)
+    for piece in early:
+        gather.from_side(piece)
+    vectors[...] = jnp.concatenate([vector_blocks[block, 0:8, 0:share] for block in range(ways)], axis=1)
+    bias[...] = jnp.concatenate(
+        [unfold(vector_blocks[block, 8:16], wide_share) for block in range(ways)], axis=1
+    )
     load_own.wait()
+    for piece in late:
+        gather.from_levels(piece, levels - 1)
+        gather.from_across(piece, levels - 2)
+    for piece in (3, *late):
+        gather.from_across(piece, levels - 1)
+    gather.from_side(3)
+    for piece in late:
+        gather.from_side(piece)
+    for piece in range(count):
+        gather.drain(piece)
 
     chunks = []
     part_refs = [vector_blocks, attend_blocks, merge_blocks, up_blocks, down_blocks]
@@ -689,25 +741,26 @@
     def down_gradient():
         def pair_at(index):
             late = lax.div(index, levels)
-            return lax.rem(index, levels), jnp.where(late == 0, 1 - place.row, place.row), late == 0
+            level = down_a.level_at(lax.rem(index, levels))
+            return level, jnp.where(late == 0, 1 - place.row, place.row), late == 0
 
         def multiply(index):
             level, row, _ = pair_at(index)
             pair = level * 2 + row
             at = pl.ds(pl.multiple_of(pair * 2 * wide_share, 128), 2 * wide_share)
             tile = flat(activated[:, :, at])
-            for chunk in (down_a, down_b):
-                at = pl.ds(chunk.start, chunk.cols)
-                product = matmul(tile, flat(entry[back, :, :, at]), TN).astype(BF)
-                for core in range(2):
-                    down_blocks[pair * 2 + core, :, at] = product[core * wide_share : (core + 1) * wide_share]
+            product = matmul(tile, flat(entry[back]), TN).astype(BF)
+            for core in range(2):
+                down_blocks[pair * 2 + core] = product[core * wide_share : (core + 1) * wide_share]
+            for chunk in (down_b, down_a):
                 chunk.side(pair).start()
 
         def join(index):
             level, row, early = pair_at(index)
-            down_a.join_pair(level, row)
             down_b.join_pair(level, row)
             pl.when(early)(down_b.across(level, level).start)
+            down_a.join_pair(level, row)
+            down_a.chain_open(row, jnp.where(early, 1, 0), level)
 
         multiply(jnp.int32(0))
 
@@ -717,36 +770,7 @@
             join(index - 1)
 
         join(jnp.int32(2 * levels - 1))
-        down_a.chain_start()
-
-    @pl.loop(0, 2 * batches)
-    def _(step):
-        is_forward = jnp.where(section == 0, step < batches, lax.rem(step, 2) == 0)
-        batch = jnp.where(section == 0, lax.rem(step, batches), lax.div(step, 2))
-
-        slot = jnp.where(section == 0, lax.rem(batch, 2), jnp.where(is_forward, 0, 1))
-
-        @pl.when(is_forward)
-        def _():
-            pl.when(section == 1)(relay(batch).wait_recv)
-            pl.when(jnp.logical_and(section == 0, batch >= 2))(relay(batch - 2).wait_send)
-            pl.when(jnp.logical_and(section == 1, batch >= 1))(keep(batch - 1).wait)
-            forward(batch, slot)
-            pl.when(section == 0)(relay(batch, slot).start)
-            pl.when(section == 1)(keep(batch, slot).start)
-
-        @pl.when(jnp.logical_not(is_forward))
-        def _():
-            pl.when(section == 0)(relay(batch).wait_recv)
-            pl.when(jnp.logical_and(section == 0, batch < 2))(relay(batch + batches - 2).wait_send)
-            pl.when(jnp.logical_and(section == 0, batch >= 2))(keep(batch - 2).wait)
-            pl.when(jnp.logical_and(section == 1, batch >= 1))(relay(batch - 1).wait_send)
-            last = jnp.logical_and(section == 0, step == 2 * batches - 1)
-            backward(batch, slot, lambda: pl.when(last)(down_gradient))
-            pl.when(section == 1)(relay(batch, slot).start)
-            pl.when(section == 0)(keep(batch, slot).start)
-
-    pl.when(section == 1)(down_gradient)
+
     stores = []
 
     def store(target, chunk, through=None, first=0):
@@ -775,7 +799,7 @@
         return target
 
     def columns(left, source, chunk, credit=None):
-        step = 128 * max(d for d in (1, 2, 3) if chunk.cols % (128 * d) == 0)
+        step = STEP if chunk.cols % STEP == 0 else chunk.cols
 
         @pl.loop(0, chunk.cols // step)
         def _(index):
@@ -792,48 +816,84 @@
             free_sem.at[index], inc=1, device_id=(section, place.targets[SIDE]), device_id_type=MESH
         )
 
+    def up_gradient():
+        turned = turn(normed_two, 0)
+        columns(turned, slope, up_a)
+        columns(turned, slope, up_b)
+        up_a.join_side()
+        release(0)
+        down_b.join_across()
+        up_b.join_side()
+        release(1)
+
+    @pl.loop(0, portions)
+    def _(portion):
+        pl.when(section == 1)(relay_part(0, portion).wait_recv)
+        forward(0, pl.multiple_of(portion * half, length), half, 0)
+        pl.when(section == 0)(relay_part(0, portion).start)
+
+    pl.when(section == 1)(keep(0).start)
+
+    @pl.loop(1, 2 * batches)
+    def _(step):
+        is_forward = jnp.where(section == 0, step < batches, lax.rem(step, 2) == 0)
+        batch = jnp.where(section == 0, lax.rem(step, batches), lax.div(step, 2))
+        slot = jnp.where(section == 0, lax.rem(batch, 2), jnp.where(is_forward, 0, 1))
+
+        def when(*conditions):
+            return pl.when(functools.reduce(jnp.logical_and, conditions))
+
+        @pl.when(is_forward)
+        def _():
+            pl.when(section == 1)(lambda: relay(batch).wait_recv())
+            when(section == 0, batch >= 2)(lambda: relay(batch - 2).wait_send())
+            pl.when(section == 1)(lambda: keep(batch - 1).wait())
+            forward(batch, 0, rows, slot)
+            pl.when(section == 0)(lambda: relay(batch, slot).start())
+            pl.when(section == 1)(lambda: keep(batch, slot).start())
+
+        @pl.when(jnp.logical_not(is_forward))
+        def _():
+            pl.when(section == 0)(lambda: relay(batch).wait_recv())
+            when(section == 0, batch < 2)(lambda: relay(batch + batches - 2).wait_send())
+            when(section == 0, batch >= 2)(lambda: keep(batch - 2).wait())
+            when(section == 1, batch >= 1)(lambda: relay(batch - 1).wait_send())
+            backward(batch, 0, rows, slot)
+            pl.when(section == 1)(lambda: relay(batch, slot).start())
+            pl.when(section == 0)(lambda: keep(batch, slot).start())
+
+    down_gradient()
+    up_gradient()
+
     for block in range(ways):
         vector_blocks[block, 0:8] = pad_lanes(vector_sum[:, block * share : (block + 1) * share])
         vector_blocks[block, 8:16] = fold(bias_sum[:, block * wide_share : (block + 1) * wide_share])
     vector.send_side()
-    turned = turn(normed_two, 0)
-    columns(turned, slope, up_a)
-    columns(turned, slope, up_b)
-    vector.join_side()
-    up_a.join_side()
-    release(0)
     down_a.chain_pass(1)
-    up_b.join_side()
-    release(1)
     turned = turn(normed, 1)
     columns(turned, projected, attend_a, 0)
+    vector.join_side()
     down_a.chain_pass(2)
-    down_b.join_across()
-    down_b.chain_start()
-    vector.join_across()
-    vector.chain_start()
+    down_b.chain_pass(1)
     columns(turned, projected, attend_b, 1)
     attend_a.join_side()
     release(2)
+    up_a.join_across()
     turned = turn(attended, 0)
     columns(turned, middle, merge, 2)
     attend_b.join_side()
-    down_b.chain_pass(1)
+    down_a.chain_end(None)
     merge.join_side()
-    down_a.chain_end(None)
-    up_a.join_across()
-    up_a.chain_start()
+    vector.join_across()
+    up_b.join_across()
     down_b.chain_pass(2)
     vector.chain_pass(1)
     up_a.chain_pass(1)
-    up_b.join_across()
-    up_b.chain_start()
     vector.chain_pass(2)
     down_b.chain_end(store(down_out, down_b))
     up_a.chain_pass(2)
+    attend_a.join_across()
     up_b.chain_pass(1)
-    attend_a.join_across()
-    attend_a.chain_start()
 
     def store_vectors(value):
         gain_out[...] = value[0:2, :share]
@@ -844,14 +904,12 @@
     vector.chain_end(store_vectors)
     up_a.chain_end(store(up_out, up_a, temp, 0))
     up_b.chain_pass(2)
+    attend_b.join_across()
     attend_a.chain_pass(1)
-    attend_b.join_across()
-    attend_b.chain_start()
     up_b.chain_end(store(up_out, up_b, temp, 0))
     attend_a.chain_pass(2)
+    merge.join_across()
     attend_b.chain_pass(1)
-    merge.join_across()
-    merge.chain_start()
     attend_a.chain_end(store(attend_out, attend_a, sum_temp, 0))
     attend_b.chain_pass(2)
     merge.chain_pass(1)
@@ -902,8 +960,8 @@
         (4, width // 2, ACROSS_FIRST, wide_share, width // 2, BF, None),
         (3, 0, ACROSS_FIRST, share, wide // 2, BF, None),
         (3, wide // 2, ACROSS_FIRST, share, wide // 2, BF, None),
-        (1, 0, ACROSS_FIRST, share, 3 * width // 2, BF, 2),
-        (1, 3 * width // 2, ACROSS_FIRST, share, 3 * width // 2, BF, 3),
+        (1, 0, ACROSS_FIRST, share, 2 * width, BF, 2),
+        (1, 2 * width, ACROSS_FIRST, share, width, BF, 3),
         (2, 0, ACROSS_FIRST, share, width, BF, 2),
         (0, 0, ACROSS_FIRST, 16, 128, F32, None),
     ]
@@ -941,8 +999,8 @@
         dma((6, 2 * levels + 1)),
         dma((6,)),
         dma(()),
-        dma((batches,)),
-        dma((batches,)),
+        dma((batches, 2)),
+        dma((batches, 2)),
         dma((batches,)),
         pltpu.SemaphoreType.REGULAR((3,)),
         dma((9,)),

time: 266 us -> 257 us (0.966)
  Pallas kernels: 265 us -> 256 us
    pallas_call x1, Pallas kernels: 262 us -> 253 us  [train_step(): pl.pallas_call(functools.partial(relay_kernel, levels, clips, plan), out_...]
where the time goes in v3:
time: 257 us
  Pallas kernels  256 us (100%)
    pallas_call x1, Pallas kernels, train_step(): pl.pallas_call(functools.partial(relay_kernel, levels, clips, plan), out_...  253 us

profile of v3, /device:TPU:0, one launch (start us, length us, event | category | flops | bytes accessed | tf_op | source)
XLA Modules:
  0.0 257.2 jit_solution(7462217200688624700)
XLA Ops:
  0.6 253.1 %shard_map.143 = (bf16[4,256,768]{2,1,0:T(8,128)(2,1)}, f32[2,48]{1,0:T(2,128)}, f32[6,1,48]{2,1,0:T(1,128)}, f32[48,2304]{1,0:T(8,128)}, f32[48,768]{1,0:T(8,12...) custom-call(bf16[4,256,768]{2,1,0:T(8,128)(2,1)} %bitcast.14, bf16[48,2304]{1,0:T(8,128)(2,1)} %bitcast.17, ...), custom_call_target="tpu_custom_call" | custom-call | tf_op jit(solution)/shard_map/pallas_call | solution.py:1014
  253.8 3.3 %shard_map.144 = (bf16[4,256,768]{2,1,0:T(8,128)(2,1)}, f32[2,48]{1,0:T(2,128)}, f32[6,1,48]{2,1,0:T(1,128)}, f32[48,2304]{1,0:T(8,128)}, f32[48,768]{1,0:T(8,12...) custom-call(bf16[4,256,768]{2,1,0:T(8,128)(2,1)} %get-tuple-element.24.refs_0_, ...), custom_call_target="tpu_custom_call" | custom-call | tf_op jit(solution)/shard_map/pallas_call | solution.py:1033

commit v4 on v3

--- a/solution.py
+++ b/solution.py
@@ -816,16 +816,6 @@
             free_sem.at[index], inc=1, device_id=(section, place.targets[SIDE]), device_id_type=MESH
         )
 
-    def up_gradient():
-        turned = turn(normed_two, 0)
-        columns(turned, slope, up_a)
-        columns(turned, slope, up_b)
-        up_a.join_side()
-        release(0)
-        down_b.join_across()
-        up_b.join_side()
-        release(1)
-
     @pl.loop(0, portions)
     def _(portion):
         pl.when(section == 1)(relay_part(0, portion).wait_recv)
@@ -863,37 +853,11 @@
             pl.when(section == 0)(lambda: keep(batch, slot).start())
 
     down_gradient()
-    up_gradient()
 
     for block in range(ways):
         vector_blocks[block, 0:8] = pad_lanes(vector_sum[:, block * share : (block + 1) * share])
         vector_blocks[block, 8:16] = fold(bias_sum[:, block * wide_share : (block + 1) * wide_share])
     vector.send_side()
-    down_a.chain_pass(1)
-    turned = turn(normed, 1)
-    columns(turned, projected, attend_a, 0)
-    vector.join_side()
-    down_a.chain_pass(2)
-    down_b.chain_pass(1)
-    columns(turned, projected, attend_b, 1)
-    attend_a.join_side()
-    release(2)
-    up_a.join_across()
-    turned = turn(attended, 0)
-    columns(turned, middle, merge, 2)
-    attend_b.join_side()
-    down_a.chain_end(None)
-    merge.join_side()
-    vector.join_across()
-    up_b.join_across()
-    down_b.chain_pass(2)
-    vector.chain_pass(1)
-    up_a.chain_pass(1)
-    vector.chain_pass(2)
-    down_b.chain_end(store(down_out, down_b))
-    up_a.chain_pass(2)
-    attend_a.join_across()
-    up_b.chain_pass(1)
 
     def store_vectors(value):
         gain_out[...] = value[0:2, :share]
@@ -901,21 +865,54 @@
             shift_out[index] = value[2 + index : 3 + index, :share]
         bias_out[...] = unfold(value[8:16], wide_share)
 
+    turned_up = turn(normed_two, 0)
+    columns(turned_up, slope, up_a)
+    up_a.join_side()
+    release(0)
+    columns(turned_up, slope, up_b)
+    down_a.chain_pass(1)
+    vector.join_side()
+    down_b.join_across()
+    turned_attend = turn(normed, 1)
+    columns(turned_attend, projected, attend_a, 0)
+    up_b.join_side()
+    release(1)
+    up_a.join_across()
+    vector.join_across()
+    down_a.chain_pass(2)
+    down_b.chain_pass(1)
+    attend_a.join_side()
+    release(2)
+    columns(turned_attend, projected, attend_b, 1)
+    turned_merge = turn(attended, 0)
+    columns(turned_merge, middle, merge, 2)
+    attend_b.join_side()
+    up_a.chain_pass(1)
+    merge.join_side()
+    up_b.join_across()
+    up_a.chain_pass(2)
+    down_b.chain_pass(2)
+    vector.chain_pass(1)
+    down_a.chain_end(None)
+    up_b.chain_pass(1)
+    up_b.chain_pass(2)
+    vector.chain_pass(2)
+    attend_a.join_across()
+    attend_a.chain_pass(1)
+    attend_b.join_across()
+    up_b.chain_end(store(up_out, up_b, temp, 0))
+    attend_b.chain_pass(1)
+    down_b.chain_end(store(down_out, down_b))
     vector.chain_end(store_vectors)
+    attend_a.chain_pass(2)
+    attend_b.chain_pass(2)
+    merge.join_across()
+    merge.chain_pass(1)
     up_a.chain_end(store(up_out, up_a, temp, 0))
-    up_b.chain_pass(2)
-    attend_b.join_across()
-    attend_a.chain_pass(1)
-    up_b.chain_end(store(up_out, up_b, temp, 0))
-    attend_a.chain_pass(2)
-    merge.join_across()
-    attend_b.chain_pass(1)
     attend_a.chain_end(store(attend_out, attend_a, sum_temp, 0))
-    attend_b.chain_pass(2)
-    merge.chain_pass(1)
-    attend_b.chain_end(store(attend_out, attend_b, sum_temp, 0))
     merge.chain_pass(2)
     down_a.finish(store(down_out, down_a))
+    attend_b.chain_end(store(attend_out, attend_b, sum_temp, 0))
     merge.chain_end(store(merge_out, merge, sum_temp, 3 * share))
     for chunk in chunks:
         chunk.drain()

time: 257 us -> 250 us (0.973)
  Pallas kernels: 256 us -> 249 us
    pallas_call x1, Pallas kernels: 253 us -> 246 us  [train_step(): pl.pallas_call(functools.partial(relay_kernel, levels, clips, plan), out_...]
where the time goes in v4:
time: 250 us
  Pallas kernels  249 us (100%)
    pallas_call x1, Pallas kernels, train_step(): pl.pallas_call(functools.partial(relay_kernel, levels, clips, plan), out_...  246 us

profile of v4, /device:TPU:0, one launch (start us, length us, event | category | flops | bytes accessed | tf_op | source)
XLA Modules:
  0.0 249.9 jit_solution(14747111963459586848)
XLA Ops:
  0.6 245.8 %shard_map.143 = (bf16[4,256,768]{2,1,0:T(8,128)(2,1)}, f32[2,48]{1,0:T(2,128)}, f32[6,1,48]{2,1,0:T(1,128)}, f32[48,2304]{1,0:T(8,128)}, f32[48,768]{1,0:T(8,12...) custom-call(bf16[4,256,768]{2,1,0:T(8,128)(2,1)} %bitcast.14, bf16[48,2304]{1,0:T(8,128)(2,1)} %bitcast.17, ...), custom_call_target="tpu_custom_call" | custom-call | tf_op jit(solution)/shard_map/pallas_call | solution.py:1011
  246.4 3.3 %shard_map.144 = (bf16[4,256,768]{2,1,0:T(8,128)(2,1)}, f32[2,48]{1,0:T(2,128)}, f32[6,1,48]{2,1,0:T(1,128)}, f32[48,2304]{1,0:T(8,128)}, f32[48,768]{1,0:T(8,12...) custom-call(bf16[4,256,768]{2,1,0:T(8,128)(2,1)} %get-tuple-element.24.refs_0_, ...), custom_call_target="tpu_custom_call" | custom-call | tf_op jit(solution)/shard_map/pallas_call | solution.py:1030

commit v5 on v4

--- a/solution.py
+++ b/solution.py
@@ -474,6 +474,27 @@
     for index in range(-(-count // 128)):
         pieces.append(rows[index : index + 1, : min(128, count - index * 128)])
     return jnp.concatenate(pieces, axis=1)
+
+
+FOUR_LEVEL_STEPS = (
+    (0, 1, 1), (4, 2, 0), (2, 2, 0), (4, 1, 1), (0, 1, 2), (2, 1, 1),
+    (5, 0, 0), (1, 1, 1), (2, 1, 2), (0, 2, 0), (3, 1, 1), (4, 2, 1),
+    (1, 1, 2), (3, 1, 2), (0, 1, 3), (0, 2, 1), (1, 1, 3), (5, 1, 1),
+    (3, 2, 0), (1, 2, 0), (1, 2, 1), (3, 1, 3), (4, 1, 2), (0, 2, 2),
+    (5, 1, 2), (3, 2, 1), (2, 1, 3), (4, 1, 3), (1, 2, 2), (0, 2, 3),
+    (2, 2, 1), (2, 2, 2), (3, 2, 2), (1, 2, 3), (2, 2, 3), (3, 2, 3),
+    (4, 2, 2), (5, 1, 3), (4, 2, 3),
+)
+
+
+def gather_steps(levels, count):
+    if levels == 4 and count == 6:
+        return FOUR_LEVEL_STEPS
+    steps = [(count - 1, 0, 0)]
+    for distance in range(1, levels):
+        for piece in range(count):
+            steps += [(piece, 1, distance), (piece, 2, distance - 1)]
+    return steps + [(piece, 2, levels - 1) for piece in range(count)]
 
 
 def relay_kernel(levels, clips, plan, *refs):
@@ -696,34 +717,22 @@
         leaving[slot, here] = (sum_temp[here] + norm_back(grad * row(0), normal, scale)).astype(BF)
 
     count = len(pieces)
-    early, late = range(3), range(4, count)
     for piece in range(count):
         gather.start(piece)
-    gather.first_across(count - 1)
-    for distance in range(1, levels - 1):
-        for piece in range(count):
+    for piece, what, distance in gather_steps(levels, count):
+        if what == 0:
+            gather.first_across(piece)
+        elif what == 1:
             gather.from_levels(piece, distance)
-            gather.from_across(piece, distance - 1)
-    for piece in range(4):
-        gather.from_levels(piece, levels - 1)
-        gather.from_across(piece, levels - 2)
-    for piece in early:
-        gather.from_across(piece, levels - 1)
-    for piece in early:
+        else:
+            gather.from_across(piece, distance)
+    for piece in range(count):
         gather.from_side(piece)
     vectors[...] = jnp.concatenate([vector_blocks[block, 0:8, 0:share] for block in range(ways)], axis=1)
     bias[...] = jnp.concatenate(
         [unfold(vector_blocks[block, 8:16], wide_share) for block in range(ways)], axis=1
     )
     load_own.wait()
-    for piece in late:
-        gather.from_levels(piece, levels - 1)
-        gather.from_across(piece, levels - 2)
-    for piece in (3, *late):
-        gather.from_across(piece, levels - 1)
-    gather.from_side(3)
-    for piece in late:
-        gather.from_side(piece)
     for piece in range(count):
         gather.drain(piece)
 

time: 250 us -> 250 us (level)
  no operation moved by 1% of the time
where the time goes in v5:
time: 250 us; the launch traced here: 249 us
  Pallas kernels  249 us (100%)
    pallas_call x1, Pallas kernels, train_step(): pl.pallas_call(functools.partial(relay_kernel, levels, clips, plan), out_...  245 us

profile of v5, /device:TPU:0, one launch (start us, length us, event | category | flops | bytes accessed | tf_op | source)
XLA Modules:
  0.0 249.4 jit_solution(9837672876481390354)
XLA Ops:
  0.6 245.3 %shard_map.143 = (bf16[4,256,768]{2,1,0:T(8,128)(2,1)}, f32[2,48]{1,0:T(2,128)}, f32[6,1,48]{2,1,0:T(1,128)}, f32[48,2304]{1,0:T(8,128)}, f32[48,768]{1,0:T(8,12...) custom-call(bf16[4,256,768]{2,1,0:T(8,128)(2,1)} %bitcast.14, bf16[48,2304]{1,0:T(8,128)(2,1)} %bitcast.17, ...), custom_call_target="tpu_custom_call" | custom-call | tf_op jit(solution)/shard_map/pallas_call | solution.py:1020
  245.9 3.3 %shard_map.144 = (bf16[4,256,768]{2,1,0:T(8,128)(2,1)}, f32[2,48]{1,0:T(2,128)}, f32[6,1,48]{2,1,0:T(1,128)}, f32[48,2304]{1,0:T(8,128)}, f32[48,768]{1,0:T(8,12...) custom-call(bf16[4,256,768]{2,1,0:T(8,128)(2,1)} %get-tuple-element.24.refs_0_, ...), custom_call_target="tpu_custom_call" | custom-call | tf_op jit(solution)/shard_map/pallas_call | solution.py:1039

commit v6 on v5

--- a/solution.py
+++ b/solution.py
@@ -107,6 +107,8 @@
         hello(self.section, self.targets[ACROSS])
         pl.when(self.has_down)(lambda: hello(self.section, self.targets[DOWN]))
         pl.when(self.has_up)(lambda: hello(self.section, self.targets[UP]))
+    def greeted(self):
+        barrier = pltpu.get_barrier_semaphore()
         ends = (self.level == 0).astype(jnp.int32) + (self.level == self.levels - 1).astype(jnp.int32)
         pl.semaphore_wait(barrier, 5 - ends)
 
@@ -545,13 +547,14 @@
     pairs = HEADS // 2
     total = batches * rows
 
+    place.greet()
     load_own = pltpu.make_async_copy(own, entry.at[0], load_sem)
     load_own.start()
     packed[0:8] = pad_lanes(
         jnp.concatenate([gain_shard[...], shift_shard[...]], axis=0).astype(F32)
     )
     packed[8:16] = fold(bias_shard[...].astype(F32))
-    place.greet()
+    place.greeted()
 
     half_share = wide_share // 2
     pieces = [

time: 250 us -> 250 us (level)
  no operation moved by 1% of the time
where the time goes in v6:
time: 250 us; the launch traced here: 249 us
  Pallas kernels  249 us (100%)
    pallas_call x1, Pallas kernels, train_step(): pl.pallas_call(functools.partial(relay_kernel, levels, clips, plan), out_...  245 us

profile of v6, /device:TPU:0, one launch (start us, length us, event | category | flops | bytes accessed | tf_op | source)
XLA Modules:
  0.0 249.4 jit_solution(14696296842776117473)
XLA Ops:
  0.6 245.3 %shard_map.143 = (bf16[4,256,768]{2,1,0:T(8,128)(2,1)}, f32[2,48]{1,0:T(2,128)}, f32[6,1,48]{2,1,0:T(1,128)}, f32[48,2304]{1,0:T(8,128)}, f32[48,768]{1,0:T(8,12...) custom-call(bf16[4,256,768]{2,1,0:T(8,128)(2,1)} %bitcast.14, bf16[48,2304]{1,0:T(8,128)(2,1)} %bitcast.17, ...), custom_call_target="tpu_custom_call" | custom-call | tf_op jit(solution)/shard_map/pallas_call | solution.py:1023
  245.9 3.3 %shard_map.144 = (bf16[4,256,768]{2,1,0:T(8,128)(2,1)}, f32[2,48]{1,0:T(2,128)}, f32[6,1,48]{2,1,0:T(1,128)}, f32[48,2304]{1,0:T(8,128)}, f32[48,768]{1,0:T(8,12...) custom-call(bf16[4,256,768]{2,1,0:T(8,128)(2,1)} %get-tuple-element.24.refs_0_, ...), custom_call_target="tpu_custom_call" | custom-call | tf_op jit(solution)/shard_map/pallas_call | solution.py:1042
